TPU v7x, 32 devices: a whole 2x2x4 slice. The times are simulated.
32 devices in a mesh: row: 4 (over y, x), col: 8 (over z, core).
Axes of the slice: x: 2, y: 2, z: 4, core: 2. Of those that a mesh axis runs over, the one named last changes fastest.
Arguments:
- pressure_guess: float32 [32, 512, 128], P('row', 'col'), may hold values from -3 to 3
- inv_density: float32 [32, 512, 128], P('row', 'col'), may hold values from 0.25 to 4
- source: float32 [32, 512, 128], P('row', 'col'), may hold values from -24 to 24
- plate_disp: float32 [16, 1024], P('row', 'col'), may hold values from -6 to 6
- plate_prev: float32 [16, 1024], P('row', 'col'), may hold values from -6 to 6
- thickness: float32 [16, 1024], P('row', 'col'), may hold values from 0.5 to 1.5
- face_owner: int32 [16384, 1], P(('row', 'col')), may hold values from 0 to 7; in each aligned block of 512 rows (0 to 511, 512 to 1023, ...) at most 128 rows name the same one
- face_elem: int32 [16384], P(('row', 'col')), may hold values from 0 to 511
- wet: int32 [16384], P(('row', 'col')), may hold values 0 or 1
Outputs:
- pressure: float32 [32, 512, 128], P('row', 'col')
- plate_next: float32 [16, 1024], P('row', 'col')
- face_motion: float32 [16384], P(('row', 'col'))
Inputs may be any that keep to these rules, and one draw needn't show every extreme that they name: `face_owner`: among the 512 faces of one device no plating device is named by more than 128 faces, and some device names one plating device exactly 128 times.
All inputs are finite; a program needn't handle non-finite values. No bound on the sum of `wet` on one device may be relied on, other than what follows from the above.
Results may differ from a plain program's by a relative error of at most 0.00002.
Values sent between devices are 32-bit elements; how exact they have to be, the bound alone decides.
A program may use at most 64 MiB of HBM per device.

v0:
```python
import jax
import jax.numpy as jnp
from jax import lax
from jax.sharding import PartitionSpec as P

SWEEPS = 3
PSTEPS = 4


OMEGA = 0.8
BEND = 0.006
LOADC = 0.25


def with_halo(cells, sides, width):
    for axis, dim in sides:
        count = lax.axis_size(axis)
        ends = count - 1
        head = lax.slice_in_dim(cells, 0, width, axis=dim)
        tail = lax.slice_in_dim(cells, cells.shape[dim] - width, cells.shape[dim], axis=dim)
        cells = jnp.concatenate(
            [
                lax.ppermute(tail, axis, [(i, (i + 1) % count) for i in range(ends)]),
                cells,
                lax.ppermute(head, axis, [((i + 1) % count, i) for i in range(ends)]),
            ],
            axis=dim,
        )
    return cells


def relax(field_ext, coeff_ext, source):
    padded_field = jnp.pad(field_ext, ((0, 0), (0, 0), (1, 1)))
    padded_coeff = jnp.pad(coeff_ext, ((0, 0), (0, 0), (1, 1)))
    center = padded_field[1:-1, 1:-1, 1:-1]
    center_coeff = padded_coeff[1:-1, 1:-1, 1:-1]
    windows = (
        (slice(2, None), slice(1, -1), slice(1, -1)),
        (slice(0, -2), slice(1, -1), slice(1, -1)),
        (slice(1, -1), slice(2, None), slice(1, -1)),
        (slice(1, -1), slice(0, -2), slice(1, -1)),
        (slice(1, -1), slice(1, -1), slice(2, None)),
        (slice(1, -1), slice(1, -1), slice(0, -2)),
    )
    diagonal = jnp.zeros_like(center)
    inflow = jnp.zeros_like(center)
    for window in windows:
        beta = 0.5 * (center_coeff + padded_coeff[window])
        diagonal = diagonal + beta
        inflow = inflow + beta * padded_field[window]
    updated = center + OMEGA * (source - (diagonal * center - inflow)) / diagonal
    return updated


def laplace(field_ext):
    return (
        field_ext[2:, 1:-1]
        + field_ext[:-2, 1:-1]
        + field_ext[1:-1, 2:]
        + field_ext[1:-1, :-2]
        - 4.0 * field_ext[1:-1, 1:-1]
    )


def bilaplace(field_ext, thick_ext):
    curvature = laplace(field_ext)
    moment = BEND * thick_ext[1:-1, 1:-1] ** 3 * curvature
    return laplace(moment)


def shards(
    pressure_guess,
    inv_density,
    source,
    plate_disp,
    plate_prev,
    thickness,
    face_owner,
    face_elem,
    wet,
):
    pressure = pressure_guess
    coeff_ext = with_halo(inv_density, (("row", 0), ("col", 1)), 1)
    for sweep_index in range(SWEEPS):
        field_ext = with_halo(pressure, (("row", 0), ("col", 1)), 1)
        pressure = relax(field_ext, coeff_ext, source)
    face_press = pressure[:, :, 0].reshape(-1)
    values = face_press * wet.astype(face_press.dtype)
    owner = face_owner[:, 0]
    elem_count = plate_disp.shape[0] * plate_disp.shape[1]
    col_count = lax.axis_size("col")
    slab_index = owner * elem_count + face_elem
    slab_vector = jax.ops.segment_sum(values, slab_index, num_segments=col_count * elem_count)
    loads = lax.psum_scatter(slab_vector, "col", scatter_dimension=0, tiled=True)
    loads = loads.reshape(plate_disp.shape)
    current = plate_disp
    previous = plate_prev
    thick_ext = with_halo(thickness, (("row", 0), ("col", 1)), 2)
    for step_index in range(PSTEPS):
        disp_ext = with_halo(current, (("row", 0), ("col", 1)), 2)
        bending = bilaplace(disp_ext, thick_ext)
        upcoming = 2.0 * current - previous + (LOADC * loads - bending) / thickness
        previous = current
        current = upcoming
    flat_disp = current.reshape(-1)
    slab_disp = lax.all_gather(flat_disp, "col", axis=0, tiled=True)
    face_motion = slab_disp[slab_index]
    return (pressure, current, face_motion)


def solution(mesh):
    placed = (
        P("row", "col", None),
        P("row", "col", None),
        P("row", "col", None),
        P("row", "col"),
        P("row", "col"),
        P("row", "col"),
        P(("row", "col"), None),
        P(("row", "col")),
        P(("row", "col")),
    )
    return jax.shard_map(
        shards,
        mesh=mesh,
        in_specs=placed,
        out_specs=(P("row", "col", None), P("row", "col"), P(("row", "col"))),
        check_vma=False,
    )
```

profile of v0, /device:TPU:0, one launch (start us, length us, event | category | flops | bytes accessed | tf_op | source)
XLA Modules:
  0.0 180.3 jit_solution(11630347460777161757)
XLA Ops:
  1.5 4.8 %collective-permute-start.1 = (f32[1,64,128]{2,1,0:T(8,128)S(1)}, f32[1,64,128]{2,1,0:T(8,128)S(1)}, u32[]{:S(2)}, u32[]{:S(2)}) collective-permute-start(f32[1,64,128]{2,1,0:T(8,128)S(1)} %get-tuple-element.17), channel_id=1, source_target_pairs={{0,8},{8,16},{16,24},{1,9},{9,17},{17,25},{2,10},{10,18},{18,26},{... | collective-permute-start | bytes 98312 | tf_op jit(solution)/shard_map/ppermute | solution.py:23
  8.4 4.5 %collective-permute-start.5 = (f32[1,64,128]{2,1,0:T(8,128)S(1)}, f32[1,64,128]{2,1,0:T(8,128)S(1)}, u32[]{:S(2)}, u32[]{:S(2)}) collective-permute-start(f32[1,64,128]{2,1,0:T(8,128)S(1)} %get-tuple-element.20), channel_id=1, source_target_pairs={{0,8},{8,16},{16,24},{1,9},{9,17},{17,25},{2,10},{10,18},{18,26},{... | collective-permute-start | bytes 98312 | tf_op jit(solution)/shard_map/ppermute | solution.py:23
  13.0 4.3 %collective-permute-start.20 = (f32[2,128]{1,0:T(2,128)S(1)}, f32[2,128]{1,0:T(2,128)S(1)}, u32[]{:S(2)}, u32[]{:S(2)}) collective-permute-start(f32[2,128]{1,0:T(2,128)S(1)} %get-tuple-element.39), channel_id=1, source_target_pairs={{0,8},{8,16},{16,24},{1,9},{9,17},{17,25},{2,10},{10,18},{18,26},{... | collective-permute-start | bytes 3080 | tf_op jit(solution)/shard_map/ppermute | solution.py:23
  22.8 4.9 %collective-permute-start.16 = (f32[2,128]{1,0:T(2,128)S(1)}, f32[2,128]{1,0:T(2,128)S(1)}, u32[]{:S(2)}, u32[]{:S(2)}) collective-permute-start(f32[2,128]{1,0:T(2,128)S(1)} %get-tuple-element.37), channel_id=1, source_target_pairs={{0,8},{8,16},{16,24},{1,9},{9,17},{17,25},{2,10},{10,18},{18,26},{... | collective-permute-start | bytes 3080 | tf_op jit(solution)/shard_map/ppermute | solution.py:23
  32.0 4.8 %collective-permute-start.3 = (f32[10,1,128]{2,1,0:T(1,128)S(1)}, f32[10,1,128]{2,1,0:T(1,128)S(1)}, u32[]{:S(2)}, u32[]{:S(2)}) collective-permute-start(f32[10,1,128]{2,1,0:T(1,128)S(1)} %get-tuple-element.9), channel_id=1, source_target_pairs={{0,1},{1,2},{2,3},{3,4},{4,5},{5,6},{6,7},{8,9},{9,10},{10,11},{11... | collective-permute-start | bytes 15368 | tf_op jit(solution)/shard_map/ppermute | solution.py:23
  38.2 4.3 %collective-permute-start.7 = (f32[10,1,128]{2,1,0:T(1,128)S(1)}, f32[10,1,128]{2,1,0:T(1,128)S(1)}, u32[]{:S(2)}, u32[]{:S(2)}) collective-permute-start(f32[10,1,128]{2,1,0:T(1,128)S(1)} %get-tuple-element.11), channel_id=1, source_target_pairs={{0,1},{1,2},{2,3},{3,4},{4,5},{5,6},{6,7},{8,9},{9,10},{10,11},{11... | collective-permute-start | bytes 15368 | tf_op jit(solution)/shard_map/ppermute | solution.py:23
  46.5 6.1 %collective-permute-start.9 = (f32[1,64,128]{2,1,0:T(8,128)S(1)}, f32[1,64,128]{2,1,0:T(8,128)S(1)}, u32[]{:S(2)}, u32[]{:S(2)}) collective-permute-start(f32[1,64,128]{2,1,0:T(8,128)S(1)} %get-tuple-element.15), channel_id=1, source_target_pairs={{0,8},{8,16},{16,24},{1,9},{9,17},{17,25},{2,10},{10,18},{18,26},{... | collective-permute-start | bytes 98312 | tf_op jit(solution)/shard_map/ppermute | solution.py:23
  55.5 4.0 %collective-permute-start.11 = (f32[10,1,128]{2,1,0:T(1,128)S(1)}, f32[10,1,128]{2,1,0:T(1,128)S(1)}, u32[]{:S(2)}, u32[]{:S(2)}) collective-permute-start(f32[10,1,128]{2,1,0:T(1,128)S(1)} %get-tuple-element.7), channel_id=1, source_target_pairs={{0,1},{1,2},{2,3},{3,4},{4,5},{5,6},{6,7},{8,9},{9,10},{10,11},{11... | collective-permute-start | bytes 15368 | tf_op jit(solution)/shard_map/ppermute | solution.py:23
  59.6 4.5 %collective-permute-start.18 = (f32[8,2]{1,0:T(8,128)S(1)}, f32[8,2]{1,0:T(8,128)S(1)}, u32[]{:S(2)}, u32[]{:S(2)}) collective-permute-start(f32[8,2]{1,0:T(8,128)S(1)} %get-tuple-element.27), channel_id=1, source_target_pairs={{0,1},{1,2},{2,3},{3,4},{4,5},{5,6},{6,7},{8,9},{9,10},{10,11},{11... | collective-permute-start | bytes 200 | tf_op jit(solution)/shard_map/ppermute | solution.py:23
  67.6 5.4 %collective-permute-start.13 = (f32[1,64,128]{2,1,0:T(8,128)S(1)}, f32[1,64,128]{2,1,0:T(8,128)S(1)}, u32[]{:S(2)}, u32[]{:S(2)}) collective-permute-start(f32[1,64,128]{2,1,0:T(8,128)S(1)} %get-tuple-element.13), channel_id=1, source_target_pairs={{0,8},{8,16},{16,24},{1,9},{9,17},{17,25},{2,10},{10,18},{18,26},{... | collective-permute-start | bytes 98312 | tf_op jit(solution)/shard_map/ppermute | solution.py:23
  76.0 3.0 %collective-permute-start.15 = (f32[10,1,128]{2,1,0:T(1,128)S(1)}, f32[10,1,128]{2,1,0:T(1,128)S(1)}, u32[]{:S(2)}, u32[]{:S(2)}) collective-permute-start(f32[10,1,128]{2,1,0:T(1,128)S(1)} %get-tuple-element.5), channel_id=1, source_target_pairs={{0,1},{1,2},{2,3},{3,4},{4,5},{5,6},{6,7},{8,9},{9,10},{10,11},{11... | collective-permute-start | bytes 15368 | tf_op jit(solution)/shard_map/ppermute | solution.py:23
  81.6 3.3 %scatter_custom_fusion = f32[4096]{0:T(1024)S(1)} fusion(s32[512]{0:T(512)S(1)} %get-tuple-element.4, f32[512]{0:T(512)S(1)} %convert_multiply_fusion, f32[]{:T(128)} %constant.11.clone.1), kind=kCustom, calls=%fused_computation.167 | custom fusion | flops 512 | bytes 16388 | tf_op jit(solution)/shard_map/scatter-add | solution.py:93
  84.8 30.5 %all-reduce.4 = f32[4096]{0:T(1024)S(1)} all-reduce(f32[4096]{0:T(1024)S(1)} %scatter_custom_fusion), channel_id=2, replica_groups=mesh['row'=4,'col'=8] {'col'}, use_global_device_ids=true, to_apply=%region_1.2.clone | all-reduce | flops 4096 | bytes 32768
  115.4 5.1 %collective-permute-start.24 = (f32[2,128]{1,0:T(2,128)S(1)}, f32[2,128]{1,0:T(2,128)S(1)}, u32[]{:S(2)}, u32[]{:S(2)}) collective-permute-start(f32[2,128]{1,0:T(2,128)S(1)} %get-tuple-element.35), channel_id=1, source_target_pairs={{0,8},{8,16},{16,24},{1,9},{9,17},{17,25},{2,10},{10,18},{18,26},{... | collective-permute-start | bytes 3080 | tf_op jit(solution)/shard_map/ppermute | solution.py:23
  121.8 5.4 %collective-permute-done.25 = f32[2,128]{1,0:T(2,128)S(1)} collective-permute-done((f32[2,128]{1,0:T(2,128)S(1)}, f32[2,128]{1,0:T(2,128)S(1)}, u32[]{:S(2)}, u32[]{:S(2)}) %collective-permute-start.25) | collective-permute-done | bytes 1056 | tf_op jit(solution)/shard_map/ppermute | solution.py:25
  131.9 4.8 %collective-permute-start.28 = (f32[2,128]{1,0:T(2,128)S(1)}, f32[2,128]{1,0:T(2,128)S(1)}, u32[]{:S(2)}, u32[]{:S(2)}) collective-permute-start(f32[2,128]{1,0:T(2,128)S(1)} %get-tuple-element.33), channel_id=1, source_target_pairs={{0,8},{8,16},{16,24},{1,9},{9,17},{17,25},{2,10},{10,18},{18,26},{... | collective-permute-start | bytes 3080 | tf_op jit(solution)/shard_map/ppermute | solution.py:23
  138.0 4.2 %collective-permute-done.29 = f32[2,128]{1,0:T(2,128)S(1)} collective-permute-done((f32[2,128]{1,0:T(2,128)S(1)}, f32[2,128]{1,0:T(2,128)S(1)}, u32[]{:S(2)}, u32[]{:S(2)}) %collective-permute-start.29) | collective-permute-done | bytes 1056 | tf_op jit(solution)/shard_map/ppermute | solution.py:25
  144.8 2.5 %collective-permute-done.31 = f32[8,2]{1,0:T(8,128)S(1)} collective-permute-done((f32[8,2]{1,0:T(8,128)S(1)}, f32[8,2]{1,0:T(8,128)S(1)}, u32[]{:S(2)}, u32[]{:S(2)}) %collective-permute-start.31) | collective-permute-done | bytes 96 | tf_op jit(solution)/shard_map/ppermute | solution.py:25
  147.6 3.0 %collective-permute-start.32 = (f32[2,128]{1,0:T(2,128)S(1)}, f32[2,128]{1,0:T(2,128)S(1)}, u32[]{:S(2)}, u32[]{:S(2)}) collective-permute-start(f32[2,128]{1,0:T(2,128)S(1)} %get-tuple-element.31), channel_id=1, source_target_pairs={{0,8},{8,16},{16,24},{1,9},{9,17},{17,25},{2,10},{10,18},{18,26},{... | collective-permute-start | bytes 3080 | tf_op jit(solution)/shard_map/ppermute | solution.py:23
  151.9 4.1 %collective-permute-done.33 = f32[2,128]{1,0:T(2,128)S(1)} collective-permute-done((f32[2,128]{1,0:T(2,128)S(1)}, f32[2,128]{1,0:T(2,128)S(1)}, u32[]{:S(2)}, u32[]{:S(2)}) %collective-permute-start.33) | collective-permute-done | bytes 1056 | tf_op jit(solution)/shard_map/ppermute | solution.py:25
  156.2 2.8 %collective-permute-start.34 = (f32[8,2]{1,0:T(8,128)S(1)}, f32[8,2]{1,0:T(8,128)S(1)}, u32[]{:S(2)}, u32[]{:S(2)}) collective-permute-start(f32[8,2]{1,0:T(8,128)S(1)} %get-tuple-element.21), channel_id=1, source_target_pairs={{0,1},{1,2},{2,3},{3,4},{4,5},{5,6},{6,7},{8,9},{9,10},{10,11},{11... | collective-permute-start | bytes 200 | tf_op jit(solution)/shard_map/ppermute | solution.py:23
  160.3 2.7 %collective-permute-done.35 = f32[8,2]{1,0:T(8,128)S(1)} collective-permute-done((f32[8,2]{1,0:T(8,128)S(1)}, f32[8,2]{1,0:T(8,128)S(1)}, u32[]{:S(2)}, u32[]{:S(2)}) %collective-permute-start.35) | collective-permute-done | bytes 96 | tf_op jit(solution)/shard_map/ppermute | solution.py:25
  163.3 12.7 %all-gather = f32[8,1,512]{2,1,0:T(1,128)S(1)} all-gather(f32[1,1,512]{2,1,0:T(1,128)S(1)} %bitcast.19), channel_id=1, replica_groups=mesh['row'=4,'col'=8] {'col'}, dimensions={0}, use_global_device_ids=true | all-gather | bytes 18432 | tf_op jit(solution)/shard_map/all_gather | solution.py:106
  176.0 4.3 %gather_fusion = f32[512]{0:T(512)} fusion(f32[4096]{0:T(1024)S(1)} %bitcast.17, s32[1024]{0:T(1024)S(1)} %pad_clamp_fusion), kind=kCustom, calls=%fused_computation | custom fusion | bytes 6144 | tf_op jit(solution)/shard_map/gather | solution.py:107
  (131 shorter events, 42.0 us)
Async XLA Ops:
  1.5 26.3 %collective-permute-start.1 = (f32[1,64,128]{2,1,0:T(8,128)S(1)}, f32[1,64,128]{2,1,0:T(8,128)S(1)}, u32[]{:S(2)}, u32[]{:S(2)}) collective-permute-start(f32[1,64,128]{2,1,0:T(8,128)S(1)} %get-tuple-element.17), channel_id=1, source_target_pairs={{0,8},{8,16},{16,24},{1,9},{9,17},{17,25},{2,10},{10,18},{18,26},{... | collective-permute-start | bytes 98312 | tf_op jit(solution)/shard_map/ppermute | solution.py:23
  6.3 22.9 %collective-permute-start = (f32[1,64,128]{2,1,0:T(8,128)S(1)}, f32[1,64,128]{2,1,0:T(8,128)S(1)}, u32[]{:S(2)}, u32[]{:S(2)}) collective-permute-start(f32[1,64,128]{2,1,0:T(8,128)S(1)} %get-tuple-element.18), channel_id=1, source_target_pairs={{8,0},{16,8},{24,16},{9,1},{17,9},{25,17},{10,2},{18,10},{26,18},{... | collective-permute-start | bytes 98312 | tf_op jit(solution)/shard_map/ppermute | solution.py:25
  8.4 22.2 %collective-permute-start.5 = (f32[1,64,128]{2,1,0:T(8,128)S(1)}, f32[1,64,128]{2,1,0:T(8,128)S(1)}, u32[]{:S(2)}, u32[]{:S(2)}) collective-permute-start(f32[1,64,128]{2,1,0:T(8,128)S(1)} %get-tuple-element.20), channel_id=1, source_target_pairs={{0,8},{8,16},{16,24},{1,9},{9,17},{17,25},{2,10},{10,18},{18,26},{... | collective-permute-start | bytes 98312 | tf_op jit(solution)/shard_map/ppermute | solution.py:23
  13.0 8.2 %collective-permute-start.20 = (f32[2,128]{1,0:T(2,128)S(1)}, f32[2,128]{1,0:T(2,128)S(1)}, u32[]{:S(2)}, u32[]{:S(2)}) collective-permute-start(f32[2,128]{1,0:T(2,128)S(1)} %get-tuple-element.39), channel_id=1, source_target_pairs={{0,8},{8,16},{16,24},{1,9},{9,17},{17,25},{2,10},{10,18},{18,26},{... | collective-permute-start | bytes 3080 | tf_op jit(solution)/shard_map/ppermute | solution.py:23
  21.2 10.8 %collective-permute-start.4 = (f32[1,64,128]{2,1,0:T(8,128)S(1)}, f32[1,64,128]{2,1,0:T(8,128)S(1)}, u32[]{:S(2)}, u32[]{:S(2)}) collective-permute-start(f32[1,64,128]{2,1,0:T(8,128)S(1)} %get-tuple-element.19), channel_id=1, source_target_pairs={{8,0},{16,8},{24,16},{9,1},{17,9},{25,17},{10,2},{18,10},{26,18},{... | collective-permute-start | bytes 98312 | tf_op jit(solution)/shard_map/ppermute | solution.py:25
  22.8 23.7 %collective-permute-start.16 = (f32[2,128]{1,0:T(2,128)S(1)}, f32[2,128]{1,0:T(2,128)S(1)}, u32[]{:S(2)}, u32[]{:S(2)}) collective-permute-start(f32[2,128]{1,0:T(2,128)S(1)} %get-tuple-element.37), channel_id=1, source_target_pairs={{0,8},{8,16},{16,24},{1,9},{9,17},{17,25},{2,10},{10,18},{18,26},{... | collective-permute-start | bytes 3080 | tf_op jit(solution)/shard_map/ppermute | solution.py:23
  27.8 24.8 %collective-permute-start.17 = (f32[2,128]{1,0:T(2,128)S(1)}, f32[2,128]{1,0:T(2,128)S(1)}, u32[]{:S(2)}, u32[]{:S(2)}) collective-permute-start(f32[2,128]{1,0:T(2,128)S(1)} %get-tuple-element.38), channel_id=1, source_target_pairs={{8,0},{16,8},{24,16},{9,1},{17,9},{25,17},{10,2},{18,10},{26,18},{... | collective-permute-start | bytes 3080 | tf_op jit(solution)/shard_map/ppermute | solution.py:25
  29.2 38.4 %collective-permute-start.22 = (f32[8,2]{1,0:T(8,128)S(1)}, f32[8,2]{1,0:T(8,128)S(1)}, u32[]{:S(2)}, u32[]{:S(2)}) collective-permute-start(f32[8,2]{1,0:T(8,128)S(1)} %get-tuple-element.29), channel_id=1, source_target_pairs={{0,1},{1,2},{2,3},{3,4},{4,5},{5,6},{6,7},{8,9},{9,10},{10,11},{11... | collective-permute-start | bytes 200 | tf_op jit(solution)/shard_map/ppermute | solution.py:23
  30.6 6.2 %collective-permute-start.2 = (f32[10,1,128]{2,1,0:T(1,128)S(1)}, f32[10,1,128]{2,1,0:T(1,128)S(1)}, u32[]{:S(2)}, u32[]{:S(2)}) collective-permute-start(f32[10,1,128]{2,1,0:T(1,128)S(1)} %get-tuple-element.10), channel_id=1, source_target_pairs={{1,0},{2,1},{3,2},{4,3},{5,4},{6,5},{7,6},{9,8},{10,9},{11,10},{12... | collective-permute-start | bytes 15368 | tf_op jit(solution)/shard_map/ppermute | solution.py:25
  32.0 6.2 %collective-permute-start.3 = (f32[10,1,128]{2,1,0:T(1,128)S(1)}, f32[10,1,128]{2,1,0:T(1,128)S(1)}, u32[]{:S(2)}, u32[]{:S(2)}) collective-permute-start(f32[10,1,128]{2,1,0:T(1,128)S(1)} %get-tuple-element.9), channel_id=1, source_target_pairs={{0,1},{1,2},{2,3},{3,4},{4,5},{5,6},{6,7},{8,9},{9,10},{10,11},{11... | collective-permute-start | bytes 15368 | tf_op jit(solution)/shard_map/ppermute | solution.py:23
  36.9 5.9 %collective-permute-start.6 = (f32[10,1,128]{2,1,0:T(1,128)S(1)}, f32[10,1,128]{2,1,0:T(1,128)S(1)}, u32[]{:S(2)}, u32[]{:S(2)}) collective-permute-start(f32[10,1,128]{2,1,0:T(1,128)S(1)} %get-tuple-element.12), channel_id=1, source_target_pairs={{1,0},{2,1},{3,2},{4,3},{5,4},{6,5},{7,6},{9,8},{10,9},{11,10},{12... | collective-permute-start | bytes 15368 | tf_op jit(solution)/shard_map/ppermute | solution.py:25
  38.2 6.0 %collective-permute-start.7 = (f32[10,1,128]{2,1,0:T(1,128)S(1)}, f32[10,1,128]{2,1,0:T(1,128)S(1)}, u32[]{:S(2)}, u32[]{:S(2)}) collective-permute-start(f32[10,1,128]{2,1,0:T(1,128)S(1)} %get-tuple-element.11), channel_id=1, source_target_pairs={{0,1},{1,2},{2,3},{3,4},{4,5},{5,6},{6,7},{8,9},{9,10},{10,11},{11... | collective-permute-start | bytes 15368 | tf_op jit(solution)/shard_map/ppermute | solution.py:23
  42.8 30.3 %collective-permute-start.23 = (f32[8,2]{1,0:T(8,128)S(1)}, f32[8,2]{1,0:T(8,128)S(1)}, u32[]{:S(2)}, u32[]{:S(2)}) collective-permute-start(f32[8,2]{1,0:T(8,128)S(1)} %get-tuple-element.30), channel_id=1, source_target_pairs={{1,0},{2,1},{3,2},{4,3},{5,4},{6,5},{7,6},{9,8},{10,9},{11,10},{12... | collective-permute-start | bytes 200 | tf_op jit(solution)/shard_map/ppermute | solution.py:25
  45.2 7.4 %collective-permute-start.8 = (f32[1,64,128]{2,1,0:T(8,128)S(1)}, f32[1,64,128]{2,1,0:T(8,128)S(1)}, u32[]{:S(2)}, u32[]{:S(2)}) collective-permute-start(f32[1,64,128]{2,1,0:T(8,128)S(1)} %get-tuple-element.16), channel_id=1, source_target_pairs={{8,0},{16,8},{24,16},{9,1},{17,9},{25,17},{10,2},{18,10},{26,18},{... | collective-permute-start | bytes 98312 | tf_op jit(solution)/shard_map/ppermute | solution.py:25
  46.5 7.7 %collective-permute-start.9 = (f32[1,64,128]{2,1,0:T(8,128)S(1)}, f32[1,64,128]{2,1,0:T(8,128)S(1)}, u32[]{:S(2)}, u32[]{:S(2)}) collective-permute-start(f32[1,64,128]{2,1,0:T(8,128)S(1)} %get-tuple-element.15), channel_id=1, source_target_pairs={{0,8},{8,16},{16,24},{1,9},{9,17},{17,25},{2,10},{10,18},{18,26},{... | collective-permute-start | bytes 98312 | tf_op jit(solution)/shard_map/ppermute | solution.py:23
  54.2 9.9 %collective-permute-start.10 = (f32[10,1,128]{2,1,0:T(1,128)S(1)}, f32[10,1,128]{2,1,0:T(1,128)S(1)}, u32[]{:S(2)}, u32[]{:S(2)}) collective-permute-start(f32[10,1,128]{2,1,0:T(1,128)S(1)} %get-tuple-element.8), channel_id=1, source_target_pairs={{1,0},{2,1},{3,2},{4,3},{5,4},{6,5},{7,6},{9,8},{10,9},{11,10},{12... | collective-permute-start | bytes 15368 | tf_op jit(solution)/shard_map/ppermute | solution.py:25
  55.5 9.9 %collective-permute-start.11 = (f32[10,1,128]{2,1,0:T(1,128)S(1)}, f32[10,1,128]{2,1,0:T(1,128)S(1)}, u32[]{:S(2)}, u32[]{:S(2)}) collective-permute-start(f32[10,1,128]{2,1,0:T(1,128)S(1)} %get-tuple-element.7), channel_id=1, source_target_pairs={{0,1},{1,2},{2,3},{3,4},{4,5},{5,6},{6,7},{8,9},{9,10},{10,11},{11... | collective-permute-start | bytes 15368 | tf_op jit(solution)/shard_map/ppermute | solution.py:23
  59.6 19.4 %collective-permute-start.18 = (f32[8,2]{1,0:T(8,128)S(1)}, f32[8,2]{1,0:T(8,128)S(1)}, u32[]{:S(2)}, u32[]{:S(2)}) collective-permute-start(f32[8,2]{1,0:T(8,128)S(1)} %get-tuple-element.27), channel_id=1, source_target_pairs={{0,1},{1,2},{2,3},{3,4},{4,5},{5,6},{6,7},{8,9},{9,10},{10,11},{11... | collective-permute-start | bytes 200 | tf_op jit(solution)/shard_map/ppermute | solution.py:23
  64.1 14.9 %collective-permute-start.19 = (f32[8,2]{1,0:T(8,128)S(1)}, f32[8,2]{1,0:T(8,128)S(1)}, u32[]{:S(2)}, u32[]{:S(2)}) collective-permute-start(f32[8,2]{1,0:T(8,128)S(1)} %get-tuple-element.28), channel_id=1, source_target_pairs={{1,0},{2,1},{3,2},{4,3},{5,4},{6,5},{7,6},{9,8},{10,9},{11,10},{12... | collective-permute-start | bytes 200 | tf_op jit(solution)/shard_map/ppermute | solution.py:25
  66.3 6.9 %collective-permute-start.12 = (f32[1,64,128]{2,1,0:T(8,128)S(1)}, f32[1,64,128]{2,1,0:T(8,128)S(1)}, u32[]{:S(2)}, u32[]{:S(2)}) collective-permute-start(f32[1,64,128]{2,1,0:T(8,128)S(1)} %get-tuple-element.14), channel_id=1, source_target_pairs={{8,0},{16,8},{24,16},{9,1},{17,9},{25,17},{10,2},{18,10},{26,18},{... | collective-permute-start | bytes 98312 | tf_op jit(solution)/shard_map/ppermute | solution.py:25
  67.6 7.1 %collective-permute-start.13 = (f32[1,64,128]{2,1,0:T(8,128)S(1)}, f32[1,64,128]{2,1,0:T(8,128)S(1)}, u32[]{:S(2)}, u32[]{:S(2)}) collective-permute-start(f32[1,64,128]{2,1,0:T(8,128)S(1)} %get-tuple-element.13), channel_id=1, source_target_pairs={{0,8},{8,16},{16,24},{1,9},{9,17},{17,25},{2,10},{10,18},{18,26},{... | collective-permute-start | bytes 98312 | tf_op jit(solution)/shard_map/ppermute | solution.py:23
  115.4 6.4 %collective-permute-start.24 = (f32[2,128]{1,0:T(2,128)S(1)}, f32[2,128]{1,0:T(2,128)S(1)}, u32[]{:S(2)}, u32[]{:S(2)}) collective-permute-start(f32[2,128]{1,0:T(2,128)S(1)} %get-tuple-element.35), channel_id=1, source_target_pairs={{0,8},{8,16},{16,24},{1,9},{9,17},{17,25},{2,10},{10,18},{18,26},{... | collective-permute-start | bytes 3080 | tf_op jit(solution)/shard_map/ppermute | solution.py:23
  120.5 6.7 %collective-permute-start.25 = (f32[2,128]{1,0:T(2,128)S(1)}, f32[2,128]{1,0:T(2,128)S(1)}, u32[]{:S(2)}, u32[]{:S(2)}) collective-permute-start(f32[2,128]{1,0:T(2,128)S(1)} %get-tuple-element.36), channel_id=1, source_target_pairs={{8,0},{16,8},{24,16},{9,1},{17,9},{25,17},{10,2},{18,10},{26,18},{... | collective-permute-start | bytes 3080 | tf_op jit(solution)/shard_map/ppermute | solution.py:25
  131.9 6.1 %collective-permute-start.28 = (f32[2,128]{1,0:T(2,128)S(1)}, f32[2,128]{1,0:T(2,128)S(1)}, u32[]{:S(2)}, u32[]{:S(2)}) collective-permute-start(f32[2,128]{1,0:T(2,128)S(1)} %get-tuple-element.33), channel_id=1, source_target_pairs={{0,8},{8,16},{16,24},{1,9},{9,17},{17,25},{2,10},{10,18},{18,26},{... | collective-permute-start | bytes 3080 | tf_op jit(solution)/shard_map/ppermute | solution.py:23
  (24 other events, 206.5 us)
where the time goes:
time: 182 us; the launch traced here: 180 us
  starting transfers between devices  94 us (52%)
  blocking collectives  43.2 us (24%)
  waiting for transfers between devices  24.6 us (14%)
  local copies, waits for them, and re-layouts  9.14 us (5%)
  other arithmetic  7.27 us (4%)
  between operations  2.11 us (1%)
    ppermute x18, starting transfers between devices, with_halo(): lax.ppermute(tail, axis, [(i, (i + 1) % count) for i in range(ends)])  70.6 us
    unnamed x1, blocking collectives  30.5 us
    ppermute x18, starting transfers between devices, with_halo(): lax.ppermute(head, axis, [((i + 1) % count, i) for i in range(ends)])  23.4 us
    ppermute x18, waiting for transfers between devices, with_halo(): lax.ppermute(head, axis, [((i + 1) % count, i) for i in range(ends)])  20.9 us
    all_gather x1, blocking collectives, shards(): slab_disp = lax.all_gather(flat_disp, 'col', axis=0, tiled=True)  12.7 us
    gather x1, local copies, waits for them, and re-layouts, shards(): face_motion = slab_disp[slab_index]  4.27 us
    ppermute x18, waiting for transfers between devices, with_halo(): lax.ppermute(tail, axis, [(i, (i + 1) % count) for i in range(ends)])  3.77 us
  transfers between devices with their start and end apart: 36, of which 10 were waited for; matrix products, arithmetic and copies ran while one was open for 2% of the time, Pallas kernels for 0%

commit v1 on v0

v1 whole, which is shorter than its diff:
```python
import functools

import jax
import jax.numpy as jnp
from jax import lax
from jax.experimental import pallas as pl
from jax.experimental.pallas import tpu as pltpu
from jax.sharding import PartitionSpec as P

SWEEPS = 3
PSTEPS = 4
OMEGA = 0.8
BEND = 0.006
LOADC = 0.25

LANES = 128
NEAR = 2
WIN = 2 * NEAR + 1
MESH = pl.DeviceIdType.MESH
NT = (((1,), (1,)), ((), ()))
F32 = jnp.float32
BF16 = jnp.bfloat16


def times(count, body):
    if count <= 32:
        for step in range(count):
            body(step)
    else:
        lax.fori_loop(0, count, lambda step, carry: (body(step), carry)[1], 0)


def three(value):
    a = value.astype(BF16)
    rest = value - a.astype(F32)
    b = rest.astype(BF16)
    c = (rest - b.astype(F32)).astype(BF16)
    return a, b, c


def kernel(
    rows, cols,
    p_ref, c_ref, s_ref, disp_ref, prev_ref, thick_ref, owner_ref, elem_ref, wet_ref,
    out_ref, plate_ref, motion_ref,
    pa, pb, wt, xrecv, ysend, yrecv,
    ibuf, vbuf, ubuf, sbuf, srecv, lslab, lrecv, win, lwin, onehot, spread, own_hot, uslab,
    fsend, frecv, gsend, grecv, tsend, trecv, rsend, rrecv,
):
    nx, ny, nz = p_ref.shape
    px, py = disp_ref.shape
    frows = owner_ref.shape[0]
    high = cols * px
    r, c = lax.axis_index("row"), lax.axis_index("col")
    last = nx - 1

    def row_ok(d):
        return jnp.logical_and(r + d >= 0, r + d < rows)

    shifts = [d for d in range(-NEAR, NEAR + 1) if d != 0]

    barrier = pltpu.get_barrier_semaphore()
    peers = cols - 1
    for d in shifts:
        @pl.when(row_ok(d))
        def _(d=d):
            pl.semaphore_signal(barrier, inc=1, device_id=(r + d, c), device_id_type=MESH)
        peers = peers + row_ok(d).astype(jnp.int32)

    def greet(step):
        pl.semaphore_signal(barrier, inc=1, device_id=(r, lax.rem(c + 1 + step, cols)), device_id_type=MESH)

    times(cols - 1, greet)

    gives = [r < rows - 1, r > 0, c < cols - 1, c > 0]
    takes = [r > 0, r < rows - 1, c > 0, c < cols - 1]
    fields = [c_ref, p_ref, pa, pb]

    def halo(phase, way):
        if way < 2:
            src = fields[phase].at[last if way == 0 else 0]
            dst = xrecv.at[phase, way]
            to = (r + 1 - 2 * way, c)
        else:
            src = ysend.at[phase, way - 2]
            dst = yrecv.at[phase, way - 2]
            to = (r, c + 1 - 2 * (way - 2))
        return pltpu.make_async_remote_copy(
            src_ref=src, dst_ref=dst, send_sem=fsend.at[phase, way], recv_sem=frecv.at[phase, way],
            device_id=to, device_id_type=MESH,
        )

    def halo_start(phase, ways):
        for way in ways:
            @pl.when(gives[way])
            def _(way=way):
                halo(phase, way).start()

    def halo_wait(phase, ways):
        for way in ways:
            @pl.when(takes[way])
            def _(way=way):
                halo(phase, way).wait_recv()

    def halo_sent(phase):
        for way in range(4):
            @pl.when(gives[way])
            def _(way=way):
                halo(phase, way).wait_send()

    def pack(phase):
        field = fields[phase]
        for x in range(nx):
            ysend[phase, 0, x:x + 1, :] = field[x, ny - 1:ny, :]
            ysend[phase, 1, x:x + 1, :] = field[x, 0:1, :]

    def gather(which, buf, step):
        return pltpu.make_async_remote_copy(
            src_ref=buf.at[c], dst_ref=buf.at[c], send_sem=gsend.at[which, step], recv_sem=grecv.at[which, step],
            device_id=(r, lax.rem(c + 1 + step, cols)), device_id_type=MESH,
        )

    def gather_start(which, buf):
        times(cols - 1, lambda step: gather(which, buf, step).start())

    def gather_wait(which, buf):
        def one(step):
            frm = lax.rem(c + cols - 1 - step, cols)
            pltpu.make_async_remote_copy(
                src_ref=buf.at[frm], dst_ref=buf.at[frm], send_sem=gsend.at[which, step],
                recv_sem=grecv.at[which, step], device_id=(r, frm), device_id_type=MESH,
            ).wait_recv()
        times(cols - 1, one)

    def gather_sent(which, buf):
        times(cols - 1, lambda step: gather(which, buf, step).wait_send())

    def beside(way):
        return pltpu.make_async_remote_copy(
            src_ref=sbuf.at[1], dst_ref=sbuf.at[2 * way], send_sem=tsend.at[way], recv_sem=trecv.at[way],
            device_id=(r, c + 1 - 2 * way), device_id_type=MESH,
        )

    def along(which, d):
        src = sbuf if which == 0 else lslab.at[pl.ds(c, 3)]
        dst = (srecv if which == 0 else lrecv).at[NEAR - d]
        return pltpu.make_async_remote_copy(
            src_ref=src, dst_ref=dst, send_sem=rsend.at[which, NEAR - d], recv_sem=rrecv.at[which, NEAR - d],
            device_id=(r + d, c), device_id_type=MESH,
        )

    def along_each(which, act, back=False):
        for d in shifts:
            @pl.when(row_ok(-d if back else d))
            def _(d=d):
                act(along(which, d))

    pack(0)
    pack(1)
    ibuf[c] = owner_ref[...] * (px * py) + elem_ref[...]
    sbuf[1, 0] = disp_ref[...]
    sbuf[1, 1] = prev_ref[...]
    sbuf[1, 2] = thick_ref[...]
    for way in range(4):
        @pl.when(jnp.logical_not(takes[way]))
        def _(way=way):
            if way < 2:
                for phase in range(4):
                    xrecv[phase, way] = jnp.zeros((ny, nz), F32)
            else:
                for phase in range(4):
                    yrecv[phase, way - 2] = jnp.zeros((nx, nz), F32)
                sbuf[2 * (way - 2)] = jnp.zeros((3, px, py), F32)
    for d in shifts:
        @pl.when(jnp.logical_not(row_ok(d)))
        def _(d=d):
            srecv[NEAR + d] = jnp.zeros(srecv.shape[1:], F32)
            lrecv[NEAR + d] = jnp.zeros(lrecv.shape[1:], F32)
    lslab[0] = jnp.zeros((px, py), F32)
    lslab[cols + 1] = jnp.zeros((px, py), F32)

    pl.semaphore_wait(barrier, peers)

    halo_start(0, (0, 1))
    halo_start(1, (0, 1))
    halo_start(0, (2, 3))
    halo_start(1, (2, 3))
    for way in range(2):
        @pl.when(gives[2 + way])
        def _(way=way):
            beside(way).start()
    gather_start(0, ibuf)

    row_id = lax.broadcasted_iota(jnp.int32, (ny, nz), 0)
    lane_id = lax.broadcasted_iota(jnp.int32, (ny, nz), 1)

    def around(plane, phase, x):
        low = jnp.where(row_id == 0, yrecv[phase, 0, x:x + 1, :], pltpu.roll(plane, 1, 0))
        up = jnp.where(row_id == ny - 1, yrecv[phase, 1, x:x + 1, :], pltpu.roll(plane, ny - 1, 0))
        left = jnp.where(lane_id == 0, 0.0, pltpu.roll(plane, 1, 1))
        right = jnp.where(lane_id == nz - 1, 0.0, pltpu.roll(plane, nz - 1, 1))
        return low, up, left, right

    def beneath(field, phase, x):
        return (
            field[x - 1] if x > 0 else xrecv[phase, 0],
            field[x + 1] if x < last else xrecv[phase, 1],
        )

    def coefficients(x):
        mid = c_ref[x]
        six = beneath(c_ref, 0, x) + around(mid, 0, x)
        diag = 3.0 * mid + 0.5 * (((six[0] + six[1]) + (six[2] + six[3])) + (six[4] + six[5]))
        scale = OMEGA / diag
        half = 0.5 * scale
        wt[0, x] = scale * s_ref[x]
        for i in range(6):
            wt[1 + i, x] = half * (mid + six[i])

    def sweep(src, dst, phase, x):
        mid = src[x]
        six = beneath(src, phase, x) + around(mid, phase, x)
        total = (1.0 - OMEGA) * mid + wt[0, x]
        for i in range(6):
            total = total + wt[1 + i, x] * six[i]
        dst[x] = total

    halo_wait(0, (2, 3))
    for x in range(1, last):
        coefficients(x)
    halo_wait(1, (2, 3))
    for x in range(1, last):
        sweep(p_ref, pa, 1, x)
    halo_wait(0, (0, 1))
    for x in (0, last):
        coefficients(x)
    halo_wait(1, (0, 1))
    for x in (0, last):
        sweep(p_ref, pa, 1, x)
    halo_start(2, (0, 1))
    pack(2)
    halo_start(2, (2, 3))

    for way in range(2):
        @pl.when(takes[2 + way])
        def _(way=way):
            beside(way).wait_recv()
    along_each(0, lambda copy: copy.start())

    halo_wait(2, (2, 3))
    for x in range(1, last):
        sweep(pa, pb, 2, x)
    halo_wait(2, (0, 1))
    for x in (0, last):
        sweep(pa, pb, 2, x)
    halo_start(3, (0, 1))
    pack(3)
    halo_start(3, (2, 3))

    gather_wait(0, ibuf)
    lo_id = lax.broadcasted_iota(jnp.int32, (py, LANES), 0)
    hi_id = lax.broadcasted_iota(jnp.int32, (high, LANES), 0)

    def mark(dev, j):
        place = lax.rem(ibuf[dev, j:j + 1, :], py)
        return jnp.where(lo_id == place, 1.0, 0.0).astype(BF16)

    def hot(dev):
        for j in range(frows):
            onehot[dev, :, j * LANES:(j + 1) * LANES] = mark(dev, j)

    times(cols, hot)
    for j in range(frows):
        own_hot[:, j * LANES:(j + 1) * LANES] = mark(c, j)

    along_each(0, lambda copy: copy.wait_recv(), back=True)
    tall = win.shape[1]
    win[:, WIN * px:, :] = jnp.zeros((3, tall - WIN * px, 3 * py), F32)
    for w in range(WIN):
        for k in range(3):
            for f in range(3):
                block = sbuf[k, f] if w == NEAR else srecv[w, k, f]
                win[f, w * px:(w + 1) * px, k * py:(k + 1) * py] = block
    current, previous, thick = win[0], win[1], win[2]
    inside = thick > 0.0
    inverse = jnp.where(inside, 1.0 / jnp.where(inside, thick, 1.0), 0.0)
    stiff = BEND * (thick * thick * thick)

    def laplace(u):
        return (
            pltpu.roll(u, 1, 0) + pltpu.roll(u, tall - 1, 0)
            + pltpu.roll(u, 1, 1) + pltpu.roll(u, 3 * py - 1, 1) - 4.0 * u
        )

    def free(now, before):
        return 2.0 * now - before - laplace(stiff * laplace(now)) * inverse

    ahead = free(current, previous)

    halo_wait(3, (2, 3))
    for x in range(1, last):
        sweep(pb, out_ref, 3, x)
    halo_wait(3, (0, 1))
    for x in (0, last):
        sweep(pb, out_ref, 3, x)

    first = (lax.broadcasted_iota(jnp.int32, (8, nz), 1) == 0).astype(F32)
    field = out_ref[...].reshape(nx * ny, nz)
    face = lax.dot_general(first, field, NT, precision=lax.Precision.HIGHEST, preferred_element_type=F32)
    for j in range(frows):
        vbuf[c, j:j + 1, :] = face[0:1, j * LANES:(j + 1) * LANES] * wet_ref[j:j + 1, :].astype(F32)
    gather_start(1, vbuf)
    gather_wait(1, vbuf)

    chunk = spread.shape[0]
    loads = jnp.zeros((3 * high, py), F32)
    for base in range(0, cols, chunk):
        def fill(dev):
            for j in range(frows):
                level = lax.div(ibuf[base + dev, j:j + 1, :], py)
                keep = hi_id == level
                for part, v in enumerate(three(vbuf[base + dev, j:j + 1, :])):
                    tile = jnp.where(keep, v.astype(F32), 0.0).astype(BF16)
                    spread[dev, part * high:(part + 1) * high, j * LANES:(j + 1) * LANES] = tile

        times(chunk, fill)
        for dev in range(chunk):
            loads = loads + lax.dot_general(
                spread[dev], onehot[base + dev], NT, preferred_element_type=F32
            )
    slab = loads[:high] + loads[high:2 * high] + loads[2 * high:]
    for dev in range(cols):
        lslab[1 + dev] = slab[dev * px:(dev + 1) * px]
    along_each(1, lambda copy: copy.start())
    along_each(1, lambda copy: copy.wait_recv(), back=True)
    lwin[WIN * px:, :] = jnp.zeros((tall - WIN * px, 3 * py), F32)
    for w in range(WIN):
        for k in range(3):
            block = lslab[c + k] if w == NEAR else lrecv[w, k]
            lwin[w * px:(w + 1) * px, k * py:(k + 1) * py] = block
    push = LOADC * lwin[...] * inverse

    previous, current = current, ahead + push
    for _ in range(PSTEPS - 1):
        previous, current = current, free(current, previous) + push
    mine = current[NEAR * px:(NEAR + 1) * px, py:2 * py]
    plate_ref[...] = mine
    ubuf[c] = mine
    gather_start(2, ubuf)
    gather_wait(2, ubuf)

    for dev in range(cols):
        uslab[dev * px:(dev + 1) * px, :] = ubuf[dev]
    parts = three(uslab[...])
    picked = lax.dot_general(
        jnp.concatenate(parts, axis=0), own_hot[...], (((1,), (0,)), ((), ())), preferred_element_type=F32
    )
    picked = picked[:high] + picked[high:2 * high] + picked[2 * high:]
    for j in range(frows):
        level = lax.div(ibuf[c, j:j + 1, :], py)
        part = jnp.where(hi_id == level, picked[:, j * LANES:(j + 1) * LANES], 0.0)
        motion_ref[j:j + 1, :] = jnp.sum(part, axis=0, keepdims=True)

    for phase in range(4):
        halo_sent(phase)
    for way in range(2):
        @pl.when(gives[2 + way])
        def _(way=way):
            beside(way).wait_send()
    for which, buf in enumerate((ibuf, vbuf, ubuf)):
        gather_sent(which, buf)
    for which in range(2):
        along_each(which, lambda copy: copy.wait_send())


def shards(rows, cols, pressure, density, source, disp, prev, thick, owner, elem, wet):
    nx, ny, nz = pressure.shape
    px, py = disp.shape
    faces = elem.shape[0]
    frows = faces // LANES
    high = cols * px
    tall = -(-WIN * px // 8) * 8
    chunk = 8 if cols % 8 == 0 else 1
    vmem = pl.BlockSpec(memory_space=pltpu.VMEM)
    dma = pltpu.SemaphoreType.DMA
    pressure, plate, motion = pl.pallas_call(
        functools.partial(kernel, rows, cols),
        out_shape=(
            jax.ShapeDtypeStruct(pressure.shape, F32),
            jax.ShapeDtypeStruct(disp.shape, F32),
            jax.ShapeDtypeStruct((frows, LANES), F32),
        ),
        in_specs=[vmem] * 9,
        out_specs=(vmem,) * 3,
        scratch_shapes=[
            pltpu.VMEM((nx, ny, nz), F32),
            pltpu.VMEM((nx, ny, nz), F32),
            pltpu.VMEM((7, nx, ny, nz), F32),
            pltpu.VMEM((4, 2, ny, nz), F32),
            pltpu.VMEM((4, 2, nx, nz), F32),
            pltpu.VMEM((4, 2, nx, nz), F32),
            pltpu.VMEM((cols, frows, LANES), jnp.int32),
            pltpu.VMEM((cols, frows, LANES), F32),
            pltpu.VMEM((cols, px, py), F32),
            pltpu.VMEM((3, 3, px, py), F32),
            pltpu.VMEM((WIN, 3, 3, px, py), F32),
            pltpu.VMEM((cols + 2, px, py), F32),
            pltpu.VMEM((WIN, 3, px, py), F32),
            pltpu.VMEM((3, tall, 3 * py), F32),
            pltpu.VMEM((tall, 3 * py), F32),
            pltpu.VMEM((cols, py, faces), BF16),
            pltpu.VMEM((chunk, 3 * high, faces), BF16),
            pltpu.VMEM((py, faces), BF16),
            pltpu.VMEM((high, py), F32),
            dma((4, 4)), dma((4, 4)),
            dma((3, cols - 1)), dma((3, cols - 1)),
            dma((2,)), dma((2,)),
            dma((2, WIN)), dma((2, WIN)),
        ],
        compiler_params=pltpu.CompilerParams(
            collective_id=0, has_side_effects=True, vmem_limit_bytes=48 * 1024 * 1024
        ),
        name="slamming",
    )(
        pressure, density, source, disp, prev, thick,
        owner.reshape(frows, LANES), elem.reshape(frows, LANES), wet.reshape(frows, LANES),
    )
    return pressure, plate, motion.reshape(faces)


def solution(mesh):
    rows, cols = mesh.shape["row"], mesh.shape["col"]
    placed = (
        P("row", "col", None),
        P("row", "col", None),
        P("row", "col", None),
        P("row", "col"),
        P("row", "col"),
        P("row", "col"),
        P(("row", "col"), None),
        P(("row", "col")),
        P(("row", "col")),
    )
    return jax.shard_map(
        functools.partial(shards, rows, cols),
        mesh=mesh,
        in_specs=placed,
        out_specs=(P("row", "col", None), P("row", "col"), P(("row", "col"))),
        check_vma=False,
    )
```

time: 182 us -> 39.7 us (0.22)
  starting transfers between devices: 94 us -> 0 us
  blocking collectives: 43.2 us -> 0 us
  Pallas kernels: 0 us -> 30.6 us
  waiting for transfers between devices: 24.6 us -> 0 us
  other arithmetic: 7.27 us -> 0 us
    ppermute x36 -> x0, starting transfers between devices: 94 us -> none  [the longest x18 70.6 us: with_halo(): lax.ppermute(tail, axis, [(i, (i + 1) % count) for i in range(ends)])]
    pallas_call x0 -> x1, Pallas kernels: none -> 30.6 us  [shards(): pl.pallas_call(functools.partial(kernel, rows, cols), out_shape=(jax.Shap...]
    unnamed x1 -> x0, blocking collectives: 30.5 us -> none
    ppermute x36 -> x0, waiting for transfers between devices: 24.6 us -> none  [the longest x18 20.9 us: with_halo(): lax.ppermute(head, axis, [((i + 1) % count, i) for i in range(ends)])]
    all_gather x1 -> x0, blocking collectives: 12.7 us -> none  [shards(): slab_disp = lax.all_gather(flat_disp, 'col', axis=0, tiled=True)]
    unnamed x29 -> x21, local copies, waits for them, and re-layouts: 2.6 us -> 8.12 us
    gather x1 -> x0, local copies, waits for them, and re-layouts: 4.27 us -> none  [shards(): face_motion = slab_disp[slab_index]]
    scatter-add x1 -> x0, other arithmetic: 3.25 us -> none  [shards(): jax.ops.segment_sum(values, slab_index, num_segments=col_count * elem_count)]
  transfers between devices with their start and end apart: 36 -> 0, of which waited for: 10 -> 0; matrix products, arithmetic and copies ran while one was open for 2% -> 0% of each run, Pallas kernels for 0% -> 0%
where the time goes in v1:
time: 39.7 us; the launch traced here: 39.4 us
  Pallas kernels  30.6 us (77%)
  local copies, waits for them, and re-layouts  8.12 us (20%)
  between operations  0.67 us (2%)
    pallas_call x1, Pallas kernels, shards(): pl.pallas_call(functools.partial(kernel, rows, cols), out_shape=(jax.Shap...  30.6 us
    unnamed x21, local copies, waits for them, and re-layouts  8.12 us

profile of v1, /device:TPU:0, one launch (start us, length us, event | category | flops | bytes accessed | tf_op | source)
XLA Modules:
  0.0 39.4 jit_solution(8787253944588474860)
XLA Ops:
  0.6 0.0 copy-start.4
  0.6 0.0 copy-start.3
  0.7 0.7 %copy-done.4 = f32[4,128]{1,0:T(4,128)S(1)} copy-done((f32[4,128]{1,0:T(4,128)S(1)}, f32[4,128]{1,0:T(4,128)}, u32[]{:S(2)}) %copy-start.4) | copy-done | bytes 2072
  1.3 0.0 copy-done.3
  1.3 0.0 copy-start
  1.3 0.9 %copy-done = f32[8,64,128]{2,1,0:T(8,128)S(1)} copy-done((f32[8,64,128]{2,1,0:T(8,128)S(1)}, f32[8,64,128]{2,1,0:T(8,128)}, u32[]{:S(2)}) %copy-start) | copy-done | bytes 262168
  2.3 0.0 copy-start.1
  2.3 0.9 %copy-done.1 = f32[8,64,128]{2,1,0:T(8,128)S(1)} copy-done((f32[8,64,128]{2,1,0:T(8,128)S(1)}, f32[8,64,128]{2,1,0:T(8,128)}, u32[]{:S(2)}) %copy-start.1) | copy-done | bytes 262168
  3.2 0.0 copy-start.2
  3.2 0.9 %copy-done.2 = f32[8,64,128]{2,1,0:T(8,128)S(1)} copy-done((f32[8,64,128]{2,1,0:T(8,128)S(1)}, f32[8,64,128]{2,1,0:T(8,128)}, u32[]{:S(2)}) %copy-start.2) | copy-done | bytes 262168
  4.2 0.0 copy-start.5
  4.2 0.7 %copy-done.5 = f32[4,128]{1,0:T(4,128)S(1)} copy-done((f32[4,128]{1,0:T(4,128)S(1)}, f32[4,128]{1,0:T(4,128)}, u32[]{:S(2)}) %copy-start.5) | copy-done | bytes 2072
  4.9 0.0 copy-start.6
  4.9 0.7 %copy-done.6 = s32[512,1]{0,1:T(1,128)S(1)} copy-done((s32[512,1]{0,1:T(1,128)S(1)}, s32[512,1]{0,1:T(1,128)}, u32[]{:S(2)}) %copy-start.6) | copy-done | bytes 2072
  5.5 0.0 copy-start.7
  5.5 0.7 %copy-done.7 = s32[512]{0:T(512)S(1)} copy-done((s32[512]{0:T(512)S(1)}, s32[512]{0:T(512)}, u32[]{:S(2)}) %copy-start.7) | copy-done | bytes 2072
  6.2 0.0 copy-start.8
  6.2 0.7 %copy-done.8 = s32[512]{0:T(512)S(1)} copy-done((s32[512]{0:T(512)S(1)}, s32[512]{0:T(512)}, u32[]{:S(2)}) %copy-start.8) | copy-done | bytes 2072
  6.9 30.6 %slamming.1 = (f32[8,64,128]{2,1,0:T(8,128)S(1)}, f32[4,128]{1,0:T(4,128)S(1)}, f32[4,128]{1,0:T(4,128)S(1)}) custom-call(f32[8,64,128]{2,1,0:T(8,128)S(1)} %copy-done, f32[8,64,128]{2,1,0:T(8,128)S(1)} %copy-done.1, f32[8,64,128]{2,1,0:T(8,128)S(1)} %copy-done.2, f32[4,128]{1,0:T(4,128)S(1)} %copy-done.3, f32[4,128]{1,0:T(4,128)S(1)} %copy-done.4, ...), custom_call_target="tpu_custom_call" | custom-call | tf_op jit(solution)/shard_map/slamming/pallas_call | solution.py:385
  37.5 0.7 %copy.15 = f32[8,64,128]{2,1,0:T(8,128)} copy(f32[8,64,128]{2,1,0:T(8,128)S(1)} %get-tuple-element.12) | data formatting | bytes 524288
  38.2 0.6 %copy.16 = f32[4,128]{1,0:T(4,128)} copy(f32[4,128]{1,0:T(4,128)S(1)} %get-tuple-element.13) | data formatting | bytes 4096
  38.8 0.6 %copy.17 = f32[512]{0:T(512)} copy(f32[512]{0:T(512)S(1)} %bitcast.7) | data formatting | bytes 4096
Async XLA Ops:
  0.6 0.7 %copy-start.4 = (f32[4,128]{1,0:T(4,128)S(1)}, f32[4,128]{1,0:T(4,128)}, u32[]{:S(2)}) copy-start(f32[4,128]{1,0:T(4,128)} %prev_ref.1) | copy-start | bytes 6148
  0.6 0.7 %copy-start.3 = (f32[4,128]{1,0:T(4,128)S(1)}, f32[4,128]{1,0:T(4,128)}, u32[]{:S(2)}) copy-start(f32[4,128]{1,0:T(4,128)} %disp_ref.1) | copy-start | bytes 6148
  1.3 0.9 %copy-start = (f32[8,64,128]{2,1,0:T(8,128)S(1)}, f32[8,64,128]{2,1,0:T(8,128)}, u32[]{:S(2)}) copy-start(f32[8,64,128]{2,1,0:T(8,128)} %p_ref.1) | copy-start | bytes 786436
  2.3 0.9 %copy-start.1 = (f32[8,64,128]{2,1,0:T(8,128)S(1)}, f32[8,64,128]{2,1,0:T(8,128)}, u32[]{:S(2)}) copy-start(f32[8,64,128]{2,1,0:T(8,128)} %c_ref.1) | copy-start | bytes 786436
  3.2 0.9 %copy-start.2 = (f32[8,64,128]{2,1,0:T(8,128)S(1)}, f32[8,64,128]{2,1,0:T(8,128)}, u32[]{:S(2)}) copy-start(f32[8,64,128]{2,1,0:T(8,128)} %s_ref.1) | copy-start | bytes 786436
  4.2 0.7 %copy-start.5 = (f32[4,128]{1,0:T(4,128)S(1)}, f32[4,128]{1,0:T(4,128)}, u32[]{:S(2)}) copy-start(f32[4,128]{1,0:T(4,128)} %thick_ref.1) | copy-start | bytes 6148
  4.9 0.7 %copy-start.6 = (s32[512,1]{0,1:T(1,128)S(1)}, s32[512,1]{0,1:T(1,128)}, u32[]{:S(2)}) copy-start(s32[512,1]{0,1:T(1,128)} %param.15) | copy-start | bytes 6148
  5.5 0.7 %copy-start.7 = (s32[512]{0:T(512)S(1)}, s32[512]{0:T(512)}, u32[]{:S(2)}) copy-start(s32[512]{0:T(512)} %param.16) | copy-start | bytes 6148
  6.2 0.7 %copy-start.8 = (s32[512]{0:T(512)S(1)}, s32[512]{0:T(512)}, u32[]{:S(2)}) copy-start(s32[512]{0:T(512)} %param.17) | copy-start | bytes 6148

commit v2 on v1

v2 whole, which is shorter than its diff:
```python
import functools

import jax
import jax.numpy as jnp
from jax import lax
from jax.experimental import pallas as pl
from jax.experimental.pallas import tpu as pltpu
from jax.sharding import PartitionSpec as P

SWEEPS = 3
PSTEPS = 4
OMEGA = 0.8
BEND = 0.006
LOADC = 0.25

LANES = 128
NEAR = 2
WIN = 2 * NEAR + 1
MESH = pl.DeviceIdType.MESH
NT = (((1,), (1,)), ((), ()))
F32 = jnp.float32
BF16 = jnp.bfloat16


def times(count, body):
    if count <= 32:
        for step in range(count):
            body(step)
    else:
        lax.fori_loop(0, count, lambda step, carry: (body(step), carry)[1], 0)


def three(value):
    a = value.astype(BF16)
    rest = value - a.astype(F32)
    b = rest.astype(BF16)
    c = (rest - b.astype(F32)).astype(BF16)
    return a, b, c


def kernel(
    rows, cols,
    p_hbm, c_hbm, s_hbm, disp_hbm, prev_hbm, thick_hbm, owner_hbm, elem_hbm, wet_hbm,
    out_ref, plate_ref, motion_ref,
    p_ref, c_ref, s_ref, small, faces_in,
    pa, pb, wt, xrecv, ysend, yrecv,
    thin, gbuf, vbuf, ubuf, srecv, lslab, lrecv, win, lwin, onehot, spread, own_hot, uslab,
    lsem, fsend, frecv, gsend, grecv, tsend, trecv, rsend, rrecv,
):
    nx, ny, nz = p_ref.shape
    px, py = small.shape[1:]
    frows = faces_in.shape[1]
    high = cols * px
    last = nx - 1
    reach = SWEEPS
    r, c = lax.axis_index("row"), lax.axis_index("col")

    def row_ok(d):
        return jnp.logical_and(r + d >= 0, r + d < rows)

    def both_ok(dr, dc):
        return jnp.logical_and(row_ok(dr), jnp.logical_and(c + dc >= 0, c + dc < cols))

    shifts = [d for d in range(-NEAR, NEAR + 1) if d != 0]
    corners = [(dr, dc) for dr in (-1, 1) for dc in (-1, 1)]
    blocks = [(-1, 0), (1, 0), (0, -1), (0, 1)] + corners

    loads_in = [
        (c_hbm, c_ref), (p_hbm, p_ref), (s_hbm, s_ref),
        (disp_hbm, small.at[0]), (prev_hbm, small.at[1]), (thick_hbm, small.at[2]),
        (owner_hbm, faces_in.at[0]), (elem_hbm, faces_in.at[1]), (wet_hbm, faces_in.at[2]),
    ]
    loads_in = [pltpu.make_async_copy(a, b, lsem.at[i]) for i, (a, b) in enumerate(loads_in)]
    for copy in loads_in:
        copy.start()

    barrier = pltpu.get_barrier_semaphore()
    peers = cols - 1
    for dr, dc in [(d, 0) for d in shifts] + corners:
        @pl.when(both_ok(dr, dc))
        def _(dr=dr, dc=dc):
            pl.semaphore_signal(barrier, inc=1, device_id=(r + dr, c + dc), device_id_type=MESH)
        peers = peers + both_ok(dr, dc).astype(jnp.int32)

    def greet(step):
        pl.semaphore_signal(barrier, inc=1, device_id=(r, lax.rem(c + 1 + step, cols)), device_id_type=MESH)

    times(cols - 1, greet)

    gives = [r < rows - 1, r > 0, c < cols - 1, c > 0]
    takes = [r > 0, r < rows - 1, c > 0, c < cols - 1]
    fields = [c_ref, p_ref, pa, pb]

    def halo(phase, way):
        if way < 2:
            src = fields[phase].at[last if way == 0 else 0]
            dst = xrecv.at[phase, way]
            to = (r + 1 - 2 * way, c)
        else:
            src = ysend.at[phase, way - 2]
            dst = yrecv.at[phase, way - 2]
            to = (r, c + 1 - 2 * (way - 2))
        return pltpu.make_async_remote_copy(
            src_ref=src, dst_ref=dst, send_sem=fsend.at[phase, way], recv_sem=frecv.at[phase, way],
            device_id=to, device_id_type=MESH,
        )

    def halo_start(phase, ways):
        for way in ways:
            @pl.when(gives[way])
            def _(way=way):
                halo(phase, way).start()

    def halo_wait(phase, ways):
        for way in ways:
            @pl.when(takes[way])
            def _(way=way):
                halo(phase, way).wait_recv()

    def halo_sent(phase):
        for way in range(4):
            @pl.when(gives[way])
            def _(way=way):
                halo(phase, way).wait_send()

    def pack(phase):
        field = fields[phase]
        for x in range(nx):
            ysend[phase, 0, x:x + 1, :] = field[x, ny - 1:ny, :]
            ysend[phase, 1, x:x + 1, :] = field[x, 0:1, :]

    def slot(which, dev):
        return gbuf.at[:, dev] if which == 0 else vbuf.at[dev]

    def gather(which, step):
        return pltpu.make_async_remote_copy(
            src_ref=slot(which, c), dst_ref=slot(which, c), send_sem=gsend.at[which, step],
            recv_sem=grecv.at[which, step], device_id=(r, lax.rem(c + 1 + step, cols)), device_id_type=MESH,
        )

    def gather_start(which):
        times(cols - 1, lambda step: gather(which, step).start())

    def gather_wait(which):
        def one(step):
            frm = lax.rem(c + cols - 1 - step, cols)
            pltpu.make_async_remote_copy(
                src_ref=slot(which, frm), dst_ref=slot(which, frm), send_sem=gsend.at[which, step],
                recv_sem=grecv.at[which, step], device_id=(r, frm), device_id_type=MESH,
            ).wait_recv()
        times(cols - 1, one)

    def gather_sent(which):
        times(cols - 1, lambda step: gather(which, step).wait_send())

    def along(which, d):
        src = gbuf.at[pl.ds(1, 3)] if which == 0 else lslab
        dst = (srecv if which == 0 else lrecv).at[NEAR - d]
        return pltpu.make_async_remote_copy(
            src_ref=src, dst_ref=dst, send_sem=rsend.at[which, NEAR - d], recv_sem=rrecv.at[which, NEAR - d],
            device_id=(r + d, c), device_id_type=MESH,
        )

    def along_each(which, act, back=False):
        for d in shifts:
            @pl.when(row_ok(-d if back else d))
            def _(d=d):
                act(along(which, d))

    far = {-1: (0, reach), 0: (reach, nx), 1: (reach + nx, reach)}

    def skin(dr, dc):
        first = {-1: reach, 0: reach, 1: nx}[dr]
        at, count = far[-dr]
        return pltpu.make_async_remote_copy(
            src_ref=thin.at[1, pl.ds(first, count)], dst_ref=thin.at[1 - dc, pl.ds(at, count)],
            send_sem=tsend.at[3 * dr + dc + 4], recv_sem=trecv.at[3 * dr + dc + 4],
            device_id=(r + dr, c + dc), device_id_type=MESH,
        )

    for way in range(4):
        @pl.when(jnp.logical_not(takes[way]))
        def _(way=way):
            if way < 2:
                for phase in range(4):
                    xrecv[phase, way] = jnp.zeros((ny, nz), F32)
            else:
                for phase in range(4):
                    yrecv[phase, way - 2] = jnp.zeros((nx, nz), F32)
    for dr, dc in blocks:
        @pl.when(jnp.logical_not(both_ok(dr, dc)))
        def _(dr=dr, dc=dc):
            at, count = far[dr]
            thin[1 + dc, at:at + count] = jnp.zeros((count, 8, LANES), F32)
    for d in shifts:
        @pl.when(jnp.logical_not(row_ok(d)))
        def _(d=d):
            srecv[NEAR + d] = jnp.zeros(srecv.shape[1:], F32)
            lrecv[NEAR + d] = jnp.zeros(lrecv.shape[1:], F32)

    loads_in[0].wait()
    pack(0)
    loads_in[1].wait()
    pack(1)
    loads_in[2].wait()
    depth = lax.broadcasted_iota(jnp.int32, (8, nz), 0)
    layer = lax.broadcasted_iota(jnp.int32, (8, nz), 1)
    top = jnp.logical_and(depth == layer, depth < 4).astype(F32)
    low = (depth == layer + 4).astype(F32)

    def take(which, field):
        return lax.dot_general(
            which, field[...].reshape(nx * ny, nz), NT, precision=lax.Precision.HIGHEST,
            preferred_element_type=F32,
        )

    hull = take(top, p_ref) + take(low, c_ref)
    feed = take(top, s_ref)
    near = lax.broadcasted_iota(jnp.int32, (8, LANES), 1)
    for x in range(nx):
        v = (x // 2) * LANES
        one, two = hull[:, v:v + LANES], feed[:, v:v + LANES]
        if x % 2 == 0:
            two = pltpu.roll(two, ny, 1)
        else:
            one = pltpu.roll(one, ny, 1)
        thin[1, reach + x] = jnp.where(near < ny, one, two)
    for copy in loads_in[3:]:
        copy.wait()
    gbuf[0, c] = (faces_in[0] * (px * py) + faces_in[1]).astype(F32)
    for f in range(3):
        gbuf[1 + f, c] = small[f]

    pl.semaphore_wait(barrier, peers)

    for dr, dc in blocks:
        @pl.when(both_ok(dr, dc))
        def _(dr=dr, dc=dc):
            skin(dr, dc).start()
    halo_start(0, (0, 1))
    halo_start(1, (0, 1))
    halo_start(0, (2, 3))
    halo_start(1, (2, 3))
    gather_start(0)

    row_id = lax.broadcasted_iota(jnp.int32, (ny, nz), 0)
    lane_id = lax.broadcasted_iota(jnp.int32, (ny, nz), 1)

    def around(plane, phase, x):
        low = jnp.where(row_id == 0, yrecv[phase, 0, x:x + 1, :], pltpu.roll(plane, 1, 0))
        up = jnp.where(row_id == ny - 1, yrecv[phase, 1, x:x + 1, :], pltpu.roll(plane, ny - 1, 0))
        left = jnp.where(lane_id == 0, 0.0, pltpu.roll(plane, 1, 1))
        right = jnp.where(lane_id == nz - 1, 0.0, pltpu.roll(plane, nz - 1, 1))
        return low, up, left, right

    def beneath(field, phase, x):
        return (
            field[x - 1] if x > 0 else xrecv[phase, 0],
            field[x + 1] if x < last else xrecv[phase, 1],
        )

    def weights(mid, six):
        diag = 3.0 * mid + 0.5 * (((six[0] + six[1]) + (six[2] + six[3])) + (six[4] + six[5]))
        scale = OMEGA / diag
        half = 0.5 * scale
        return scale, [half * (mid + one) for one in six]

    def coefficients(x):
        mid = c_ref[x]
        scale, six = weights(mid, beneath(c_ref, 0, x) + around(mid, 0, x))
        wt[0, x] = scale * s_ref[x]
        for i in range(6):
            wt[1 + i, x] = six[i]

    def sweep(src, dst, phase, x):
        mid = src[x]
        six = beneath(src, phase, x) + around(mid, phase, x)
        total = (1.0 - OMEGA) * mid + wt[0, x]
        for i in range(6):
            total = total + wt[1 + i, x] * six[i]
        dst[x] = total

    halo_wait(0, (2, 3))
    for x in range(1, last):
        coefficients(x)
    halo_wait(1, (2, 3))
    for x in range(1, last):
        sweep(p_ref, pa, 1, x)

    for dr, dc in blocks:
        @pl.when(both_ok(-dr, -dc))
        def _(dr=dr, dc=dc):
            skin(dr, dc).wait_recv()
    half = ny // 2
    ps, cs, ss = [], [], []
    for x in range(nx + 2 * reach):
        left, own, right = thin[0, x], thin[1, x], thin[2, x]
        side = jnp.where(near >= half, left, right)
        middle = jnp.logical_and(near >= half, near < half + ny)
        pc = jnp.where(middle, pltpu.roll(own, half, 1), pltpu.roll(side, half + ny, 1))
        side = jnp.where(near >= ny + half, left, right)
        ss.append(jnp.where(middle, pltpu.roll(own, half + ny, 1), pltpu.roll(side, half, 1)))
        ps.append(jnp.where(depth[:, :LANES] < 4, pc, 0.0))
        cs.append(jnp.where(depth[:, :LANES] < 4, pltpu.roll(pc, 4, 0), 0.0))

    def thin_six(field, x):
        mid = field[x]
        return (
            field[x - 1], field[x + 1], pltpu.roll(mid, 1, 1), pltpu.roll(mid, LANES - 1, 1),
            jnp.where(depth == 0, 0.0, pltpu.roll(mid, 1, 0)), pltpu.roll(mid, 7, 0),
        )

    shares = {}
    for x in range(1, nx + 2 * reach - 1):
        scale, six = weights(cs[x], thin_six(cs, x))
        shares[x] = (scale * ss[x], six, cs[x] > 0.0)
    for level in range(1, reach + 1):
        new = list(ps)
        for x in range(level, nx + 2 * reach - level):
            fixed, six, inside = shares[x]
            total = (1.0 - OMEGA) * ps[x] + fixed
            for a, b in zip(six, thin_six(ps, x)):
                total = total + a * b
            new[x] = jnp.where(inside, total, 0.0)
        ps = new
    for j in range(frows):
        even = pltpu.roll(ps[reach + 2 * j], LANES - half, 1)
        odd = pltpu.roll(ps[reach + 2 * j + 1], half, 1)
        face = jnp.where(near < ny, even, odd)[0:1]
        vbuf[c, j:j + 1, :] = face * faces_in[2, j:j + 1, :].astype(F32)
    gather_start(1)

    halo_wait(0, (0, 1))
    for x in (0, last):
        coefficients(x)
    halo_wait(1, (0, 1))
    for x in (0, last):
        sweep(p_ref, pa, 1, x)
    halo_start(2, (0, 1))
    pack(2)
    halo_start(2, (2, 3))

    gather_wait(0)
    along_each(0, lambda copy: copy.start())
    lo_id = lax.broadcasted_iota(jnp.int32, (py, LANES), 0)
    hi_id = lax.broadcasted_iota(jnp.int32, (high, LANES), 0)

    def index(dev, j):
        return gbuf[0, dev, j:j + 1, :].astype(jnp.int32)

    def mark(dev, j):
        return jnp.where(lo_id == lax.rem(index(dev, j), py), 1.0, 0.0).astype(BF16)

    def hot(dev):
        for j in range(frows):
            onehot[dev, :, j * LANES:(j + 1) * LANES] = mark(dev, j)

    times(cols, hot)
    for j in range(frows):
        own_hot[:, j * LANES:(j + 1) * LANES] = mark(c, j)

    gather_wait(1)
    chunk = spread.shape[0]
    loads = jnp.zeros((3 * high, py), F32)
    for base in range(0, cols, chunk):
        def fill(dev):
            for j in range(frows):
                keep = hi_id == lax.div(index(base + dev, j), py)
                for part, v in enumerate(three(vbuf[base + dev, j:j + 1, :])):
                    tile = jnp.where(keep, v.astype(F32), 0.0).astype(BF16)
                    spread[dev, part * high:(part + 1) * high, j * LANES:(j + 1) * LANES] = tile

        times(chunk, fill)
        for dev in range(chunk):
            loads = loads + lax.dot_general(
                spread[dev], onehot[base + dev], NT, preferred_element_type=F32
            )
    slab = loads[:high] + loads[high:2 * high] + loads[2 * high:]
    for dev in range(cols):
        lslab[dev] = slab[dev * px:(dev + 1) * px]
    along_each(1, lambda copy: copy.start())

    halo_wait(2, (2, 3))
    for x in range(1, last):
        sweep(pa, pb, 2, x)
    halo_wait(2, (0, 1))
    for x in (0, last):
        sweep(pa, pb, 2, x)
    halo_start(3, (0, 1))
    pack(3)
    halo_start(3, (2, 3))

    along_each(0, lambda copy: copy.wait_recv(), back=True)
    tall, wide = lwin.shape
    win[:, WIN * px:, :] = jnp.zeros((3, tall - WIN * px, wide), F32)
    for w in range(WIN):
        for k in range(cols):
            for f in range(3):
                block = gbuf[1 + f, k] if w == NEAR else srecv[w, f, k]
                win[f, w * px:(w + 1) * px, k * py:(k + 1) * py] = block
    current, previous, thick = win[0], win[1], win[2]
    present = thick > 0.0
    inverse = jnp.where(present, 1.0 / jnp.where(present, thick, 1.0), 0.0)
    stiff = BEND * (thick * thick * thick)
    across = lax.broadcasted_iota(jnp.int32, (tall, wide), 1)

    def laplace(u):
        return (
            pltpu.roll(u, 1, 0) + pltpu.roll(u, tall - 1, 0)
            + jnp.where(across == 0, 0.0, pltpu.roll(u, 1, 1))
            + jnp.where(across == wide - 1, 0.0, pltpu.roll(u, wide - 1, 1)) - 4.0 * u
        )

    def free(now, before):
        return 2.0 * now - before - laplace(stiff * laplace(now)) * inverse

    ahead = free(current, previous)

    along_each(1, lambda copy: copy.wait_recv(), back=True)
    lwin[WIN * px:, :] = jnp.zeros((tall - WIN * px, wide), F32)
    for w in range(WIN):
        for k in range(cols):
            block = lslab[k] if w == NEAR else lrecv[w, k]
            lwin[w * px:(w + 1) * px, k * py:(k + 1) * py] = block
    push = LOADC * lwin[...] * inverse
    previous, current = current, ahead + push
    for _ in range(PSTEPS - 1):
        previous, current = current, free(current, previous) + push
    for dev in range(cols):
        piece = current[NEAR * px:(NEAR + 1) * px, dev * py:(dev + 1) * py]
        ubuf[dev] = piece
        uslab[dev * px:(dev + 1) * px, :] = piece
    plate_ref[...] = ubuf[c]

    parts = three(uslab[...])
    picked = lax.dot_general(
        jnp.concatenate(parts, axis=0), own_hot[...], (((1,), (0,)), ((), ())), preferred_element_type=F32
    )
    picked = picked[:high] + picked[high:2 * high] + picked[2 * high:]
    for j in range(frows):
        keep = hi_id == lax.div(index(c, j), py)
        part = jnp.where(keep, picked[:, j * LANES:(j + 1) * LANES], 0.0)
        motion_ref[j:j + 1, :] = jnp.sum(part, axis=0, keepdims=True)

    halo_wait(3, (2, 3))
    for x in range(1, last):
        sweep(pb, out_ref, 3, x)
    halo_wait(3, (0, 1))
    for x in (0, last):
        sweep(pb, out_ref, 3, x)

    for phase in range(4):
        halo_sent(phase)
    for dr, dc in blocks:
        @pl.when(both_ok(dr, dc))
        def _(dr=dr, dc=dc):
            skin(dr, dc).wait_send()
    for which in range(2):
        gather_sent(which)
        along_each(which, lambda copy: copy.wait_send())


def write(p_ref, plate_ref, motion_ref, p_out, plate_out, motion_out, sem):
    pairs = ((p_ref, p_out), (plate_ref, plate_out), (motion_ref, motion_out))
    copies = [pltpu.make_async_copy(a, b, sem.at[i]) for i, (a, b) in enumerate(pairs)]
    for copy in copies:
        copy.start()
    for copy in copies:
        copy.wait()


def shards(rows, cols, pressure, density, source, disp, prev, thick, owner, elem, wet):
    nx, ny, nz = pressure.shape
    px, py = disp.shape
    faces = elem.shape[0]
    frows = faces // LANES
    assert LANES == 2 * ny and nz == LANES and py == LANES
    high = cols * px
    tall = -(-WIN * px // 8) * 8
    chunk = 8 if cols % 8 == 0 else 1
    vmem = pl.BlockSpec(memory_space=pltpu.VMEM)
    hbm = pl.BlockSpec(memory_space=pltpu.HBM)
    dma = pltpu.SemaphoreType.DMA
    shapes = (
        jax.ShapeDtypeStruct(pressure.shape, F32),
        jax.ShapeDtypeStruct(disp.shape, F32),
        jax.ShapeDtypeStruct((frows, LANES), F32),
    )
    tables = [x.reshape(frows, LANES) for x in (owner, elem, wet)]
    operands = [
        pltpu.with_memory_space_constraint(x, pltpu.HBM)
        for x in (pressure, density, source, disp, prev, thick, *tables)
    ]
    results = pl.pallas_call(
        functools.partial(kernel, rows, cols),
        out_shape=tuple(pltpu.VMEM(s.shape, s.dtype) for s in shapes),
        in_specs=[hbm] * 9,
        out_specs=(vmem,) * 3,
        scratch_shapes=[
            pltpu.VMEM((nx, ny, nz), F32),
            pltpu.VMEM((nx, ny, nz), F32),
            pltpu.VMEM((nx, ny, nz), F32),
            pltpu.VMEM((3, px, py), F32),
            pltpu.VMEM((3, frows, LANES), jnp.int32),
            pltpu.VMEM((nx, ny, nz), F32),
            pltpu.VMEM((nx, ny, nz), F32),
            pltpu.VMEM((7, nx, ny, nz), F32),
            pltpu.VMEM((4, 2, ny, nz), F32),
            pltpu.VMEM((4, 2, nx, nz), F32),
            pltpu.VMEM((4, 2, nx, nz), F32),
            pltpu.VMEM((3, nx + 2 * SWEEPS, 8, LANES), F32),
            pltpu.VMEM((4, cols, px, py), F32),
            pltpu.VMEM((cols, frows, LANES), F32),
            pltpu.VMEM((cols, px, py), F32),
            pltpu.VMEM((WIN, 3, cols, px, py), F32),
            pltpu.VMEM((cols, px, py), F32),
            pltpu.VMEM((WIN, cols, px, py), F32),
            pltpu.VMEM((3, tall, cols * py), F32),
            pltpu.VMEM((tall, cols * py), F32),
            pltpu.VMEM((cols, py, faces), BF16),
            pltpu.VMEM((chunk, 3 * high, faces), BF16),
            pltpu.VMEM((py, faces), BF16),
            pltpu.VMEM((high, py), F32),
            dma((9,)),
            dma((4, 4)), dma((4, 4)),
            dma((2, cols - 1)), dma((2, cols - 1)),
            dma((9,)), dma((9,)),
            dma((2, WIN)), dma((2, WIN)),
        ],
        compiler_params=pltpu.CompilerParams(
            collective_id=0, has_side_effects=True, vmem_limit_bytes=48 * 1024 * 1024
        ),
        name="slamming",
    )(*operands)
    pressure, plate, motion = pl.pallas_call(
        write,
        out_shape=shapes,
        in_specs=[vmem] * 3,
        out_specs=(hbm,) * 3,
        scratch_shapes=[dma((3,))],
        compiler_params=pltpu.CompilerParams(vmem_limit_bytes=8 * 1024 * 1024),
        name="write_results",
    )(*results)
    return pressure, plate, motion.reshape(faces)


def solution(mesh):
    rows, cols = mesh.shape["row"], mesh.shape["col"]
    placed = (
        P("row", "col", None),
        P("row", "col", None),
        P("row", "col", None),
        P("row", "col"),
        P("row", "col"),
        P("row", "col"),
        P(("row", "col"), None),
        P(("row", "col")),
        P(("row", "col")),
    )
    return jax.shard_map(
        functools.partial(shards, rows, cols),
        mesh=mesh,
        in_specs=placed,
        out_specs=(P("row", "col", None), P("row", "col"), P(("row", "col"))),
        check_vma=False,
    )
```

time: 39.7 us -> 21.9 us (0.55)
  Pallas kernels: 30.6 us -> 21.1 us
  local copies, waits for them, and re-layouts: 8.12 us -> 0 us
    pallas_call x1 -> x2, Pallas kernels: 30.6 us -> 21.1 us  [the longest x1 20.3 us: shards(): pl.pallas_call(functools.partial(kernel, rows, cols), out_shape=tuple((pl...]
    unnamed x21 -> x0, local copies, waits for them, and re-layouts: 8.12 us -> none
where the time goes in v2:
time: 21.9 us; the launch traced here: 21.7 us
  Pallas kernels  21.1 us (96%)
  between operations  0.64 us (3%)
    pallas_call x1, Pallas kernels, shards(): pl.pallas_call(functools.partial(kernel, rows, cols), out_shape=tuple((pl...  20.3 us
    pallas_call x1, Pallas kernels, shards(): pl.pallas_call(write, out_shape=shapes, in_specs=[vmem] * 3, out_specs=(h...  0.74 us

profile of v2, /device:TPU:0, one launch (start us, length us, event | category | flops | bytes accessed | tf_op | source)
XLA Modules:
  0.0 21.7 jit_solution(11387660965767107753)
XLA Ops:
  0.6 20.3 %slamming.1 = (f32[8,64,128]{2,1,0:T(8,128)S(1)}, f32[4,128]{1,0:T(4,128)S(1)}, f32[4,128]{1,0:T(4,128)S(1)}) custom-call(f32[8,64,128]{2,1,0:T(8,128)} %p_hbm.1, f32[8,64,128]{2,1,0:T(8,128)} %c_hbm.1, f32[8,64,128]{2,1,0:T(8,128)} %s_hbm.1, f32[4,128]{1,0:T(4,128)} %disp_hbm.1, f32[4,128]{1,0:T(4,128)} %prev_hbm.1, f32[4,128]{1,0:T(4,128)} %thick_hbm.1, ...), custom_call_target="tpu_custom_call" | custom-call | tf_op jit(solution)/shard_map/slamming/pallas_call | solution.py:494
  21.0 0.7 %write_results.1 = (f32[8,64,128]{2,1,0:T(8,128)}, f32[4,128]{1,0:T(4,128)}, f32[4,128]{1,0:T(4,128)}) custom-call(f32[8,64,128]{2,1,0:T(8,128)S(1)} %get-tuple-element.9.p_ref, f32[4,128]{1,0:T(4,128)S(1)} %get-tuple-element.10.plate_ref, f32[4,128]{1,0:T(4,128)S(1)} %get-tuple-element.11.motion_ref), custom_call_target="tpu_custom_call" | custom-call | tf_op jit(solution)/shard_map/write_results/pallas_call | solution.py:535

commit v3 on v2

--- a/solution.py
+++ b/solution.py
@@ -44,7 +44,7 @@
     out_ref, plate_ref, motion_ref,
     p_ref, c_ref, s_ref, small, faces_in,
     pa, pb, wt, xrecv, ysend, yrecv,
-    thin, gbuf, vbuf, ubuf, srecv, lslab, lrecv, win, lwin, onehot, spread, own_hot, uslab,
+    thin, ibuf, vbuf, ubuf, stat, lslab, lrecv, win, lwin, onehot, spread, own_hot, uslab,
     lsem, fsend, frecv, gsend, grecv, tsend, trecv, rsend, rrecv,
 ):
     nx, ny, nz = p_ref.shape
@@ -90,10 +90,11 @@
     gives = [r < rows - 1, r > 0, c < cols - 1, c > 0]
     takes = [r > 0, r < rows - 1, c > 0, c < cols - 1]
     fields = [c_ref, p_ref, pa, pb]
+    sources = [c_hbm, p_hbm, pa, pb]
 
     def halo(phase, way):
         if way < 2:
-            src = fields[phase].at[last if way == 0 else 0]
+            src = sources[phase].at[last if way == 0 else 0]
             dst = xrecv.at[phase, way]
             to = (r + 1 - 2 * way, c)
         else:
@@ -130,7 +131,7 @@
             ysend[phase, 1, x:x + 1, :] = field[x, 0:1, :]
 
     def slot(which, dev):
-        return gbuf.at[:, dev] if which == 0 else vbuf.at[dev]
+        return (ibuf, vbuf, stat)[which].at[dev]
 
     def gather(which, step):
         return pltpu.make_async_remote_copy(
@@ -154,8 +155,8 @@
         times(cols - 1, lambda step: gather(which, step).wait_send())
 
     def along(which, d):
-        src = gbuf.at[pl.ds(1, 3)] if which == 0 else lslab
-        dst = (srecv if which == 0 else lrecv).at[NEAR - d]
+        src = stat.at[c, NEAR] if which == 0 else lslab
+        dst = stat.at[c, NEAR - d] if which == 0 else lrecv.at[NEAR - d]
         return pltpu.make_async_remote_copy(
             src_ref=src, dst_ref=dst, send_sem=rsend.at[which, NEAR - d], recv_sem=rrecv.at[which, NEAR - d],
             device_id=(r + d, c), device_id_type=MESH,
@@ -195,13 +196,19 @@
     for d in shifts:
         @pl.when(jnp.logical_not(row_ok(d)))
         def _(d=d):
-            srecv[NEAR + d] = jnp.zeros(srecv.shape[1:], F32)
+            stat[c, NEAR + d] = jnp.zeros(stat.shape[2:], F32)
             lrecv[NEAR + d] = jnp.zeros(lrecv.shape[1:], F32)
 
+    pl.semaphore_wait(barrier, peers)
+
+    halo_start(0, (0, 1))
+    halo_start(1, (0, 1))
     loads_in[0].wait()
     pack(0)
+    halo_start(0, (2, 3))
     loads_in[1].wait()
     pack(1)
+    halo_start(1, (2, 3))
     loads_in[2].wait()
     depth = lax.broadcasted_iota(jnp.int32, (8, nz), 0)
     layer = lax.broadcasted_iota(jnp.int32, (8, nz), 1)
@@ -225,22 +232,15 @@
         else:
             one = pltpu.roll(one, ny, 1)
         thin[1, reach + x] = jnp.where(near < ny, one, two)
-    for copy in loads_in[3:]:
-        copy.wait()
-    gbuf[0, c] = (faces_in[0] * (px * py) + faces_in[1]).astype(F32)
-    for f in range(3):
-        gbuf[1 + f, c] = small[f]
-
-    pl.semaphore_wait(barrier, peers)
-
     for dr, dc in blocks:
         @pl.when(both_ok(dr, dc))
         def _(dr=dr, dc=dc):
             skin(dr, dc).start()
-    halo_start(0, (0, 1))
-    halo_start(1, (0, 1))
-    halo_start(0, (2, 3))
-    halo_start(1, (2, 3))
+    for copy in loads_in[3:]:
+        copy.wait()
+    stat[c, NEAR] = small[...]
+    along_each(0, lambda copy: copy.start())
+    ibuf[c] = faces_in[0] * (px * py) + faces_in[1]
     gather_start(0)
 
     row_id = lax.broadcasted_iota(jnp.int32, (ny, nz), 0)
@@ -340,13 +340,14 @@
     pack(2)
     halo_start(2, (2, 3))
 
+    along_each(0, lambda copy: copy.wait_recv(), back=True)
+    gather_start(2)
     gather_wait(0)
-    along_each(0, lambda copy: copy.start())
     lo_id = lax.broadcasted_iota(jnp.int32, (py, LANES), 0)
     hi_id = lax.broadcasted_iota(jnp.int32, (high, LANES), 0)
 
     def index(dev, j):
-        return gbuf[0, dev, j:j + 1, :].astype(jnp.int32)
+        return ibuf[dev, j:j + 1, :]
 
     def mark(dev, j):
         return jnp.where(lo_id == lax.rem(index(dev, j), py), 1.0, 0.0).astype(BF16)
@@ -358,6 +359,15 @@
     times(cols, hot)
     for j in range(frows):
         own_hot[:, j * LANES:(j + 1) * LANES] = mark(c, j)
+
+    halo_wait(2, (0, 1, 2, 3))
+    for x in (0, last):
+        sweep(pa, pb, 2, x)
+    halo_start(3, (0, 1))
+    for x in range(1, last):
+        sweep(pa, pb, 2, x)
+    pack(3)
+    halo_start(3, (2, 3))
 
     gather_wait(1)
     chunk = spread.shape[0]
@@ -380,24 +390,13 @@
         lslab[dev] = slab[dev * px:(dev + 1) * px]
     along_each(1, lambda copy: copy.start())
 
-    halo_wait(2, (2, 3))
-    for x in range(1, last):
-        sweep(pa, pb, 2, x)
-    halo_wait(2, (0, 1))
-    for x in (0, last):
-        sweep(pa, pb, 2, x)
-    halo_start(3, (0, 1))
-    pack(3)
-    halo_start(3, (2, 3))
-
-    along_each(0, lambda copy: copy.wait_recv(), back=True)
+    gather_wait(2)
     tall, wide = lwin.shape
     win[:, WIN * px:, :] = jnp.zeros((3, tall - WIN * px, wide), F32)
     for w in range(WIN):
         for k in range(cols):
             for f in range(3):
-                block = gbuf[1 + f, k] if w == NEAR else srecv[w, f, k]
-                win[f, w * px:(w + 1) * px, k * py:(k + 1) * py] = block
+                win[f, w * px:(w + 1) * px, k * py:(k + 1) * py] = stat[k, w, f]
     current, previous, thick = win[0], win[1], win[2]
     present = thick > 0.0
     inverse = jnp.where(present, 1.0 / jnp.where(present, thick, 1.0), 0.0)
@@ -415,6 +414,20 @@
         return 2.0 * now - before - laplace(stiff * laplace(now)) * inverse
 
     ahead = free(current, previous)
+
+    halo_wait(3, (2, 3))
+    for x in range(1, last):
+        sweep(pb, out_ref, 3, x)
+
+    for phase in range(3):
+        halo_sent(phase)
+    for dr, dc in blocks:
+        @pl.when(both_ok(dr, dc))
+        def _(dr=dr, dc=dc):
+            skin(dr, dc).wait_send()
+    for which in range(3):
+        gather_sent(which)
+    along_each(0, lambda copy: copy.wait_send())
 
     along_each(1, lambda copy: copy.wait_recv(), back=True)
     lwin[WIN * px:, :] = jnp.zeros((tall - WIN * px, wide), F32)
@@ -442,22 +455,11 @@
         part = jnp.where(keep, picked[:, j * LANES:(j + 1) * LANES], 0.0)
         motion_ref[j:j + 1, :] = jnp.sum(part, axis=0, keepdims=True)
 
-    halo_wait(3, (2, 3))
-    for x in range(1, last):
-        sweep(pb, out_ref, 3, x)
     halo_wait(3, (0, 1))
     for x in (0, last):
         sweep(pb, out_ref, 3, x)
-
-    for phase in range(4):
-        halo_sent(phase)
-    for dr, dc in blocks:
-        @pl.when(both_ok(dr, dc))
-        def _(dr=dr, dc=dc):
-            skin(dr, dc).wait_send()
-    for which in range(2):
-        gather_sent(which)
-        along_each(which, lambda copy: copy.wait_send())
+    halo_sent(3)
+    along_each(1, lambda copy: copy.wait_send())
 
 
 def write(p_ref, plate_ref, motion_ref, p_out, plate_out, motion_out, sem):
@@ -509,10 +511,10 @@
             pltpu.VMEM((4, 2, nx, nz), F32),
             pltpu.VMEM((4, 2, nx, nz), F32),
             pltpu.VMEM((3, nx + 2 * SWEEPS, 8, LANES), F32),
-            pltpu.VMEM((4, cols, px, py), F32),
+            pltpu.VMEM((cols, frows, LANES), jnp.int32),
             pltpu.VMEM((cols, frows, LANES), F32),
             pltpu.VMEM((cols, px, py), F32),
-            pltpu.VMEM((WIN, 3, cols, px, py), F32),
+            pltpu.VMEM((cols, WIN, 3, px, py), F32),
             pltpu.VMEM((cols, px, py), F32),
             pltpu.VMEM((WIN, cols, px, py), F32),
             pltpu.VMEM((3, tall, cols * py), F32),
@@ -523,7 +525,7 @@
             pltpu.VMEM((high, py), F32),
             dma((9,)),
             dma((4, 4)), dma((4, 4)),
-            dma((2, cols - 1)), dma((2, cols - 1)),
+            dma((3, cols - 1)), dma((3, cols - 1)),
             dma((9,)), dma((9,)),
             dma((2, WIN)), dma((2, WIN)),
         ],

time: 21.9 us -> 24.6 us (1.12)
  Pallas kernels: 21.1 us -> 23.8 us
    pallas_call x1, Pallas kernels: 20.3 us -> 23.1 us  [shards(): pl.pallas_call(functools.partial(kernel, rows, cols), out_shape=tuple((pl...]
where the time goes in v3:
time: 24.6 us; the launch traced here: 24.5 us
  Pallas kernels  23.8 us (97%)
  between operations  0.64 us (3%)
    pallas_call x1, Pallas kernels, shards(): pl.pallas_call(functools.partial(kernel, rows, cols), out_shape=tuple((pl...  23.1 us
    pallas_call x1, Pallas kernels, shards(): pl.pallas_call(write, out_shape=shapes, in_specs=[vmem] * 3, out_specs=(h...  0.74 us

profile of v3, /device:TPU:0, one launch (start us, length us, event | category | flops | bytes accessed | tf_op | source)
XLA Modules:
  0.0 24.5 jit_solution(6753044656880231918)
XLA Ops:
  0.6 23.1 %slamming.1 = (f32[8,64,128]{2,1,0:T(8,128)S(1)}, f32[4,128]{1,0:T(4,128)S(1)}, f32[4,128]{1,0:T(4,128)S(1)}) custom-call(f32[8,64,128]{2,1,0:T(8,128)} %p_hbm.1, f32[8,64,128]{2,1,0:T(8,128)} %c_hbm.1, f32[8,64,128]{2,1,0:T(8,128)} %s_hbm.1, f32[4,128]{1,0:T(4,128)} %disp_hbm.1, f32[4,128]{1,0:T(4,128)} %prev_hbm.1, f32[4,128]{1,0:T(4,128)} %thick_hbm.1, ...), custom_call_target="tpu_custom_call" | custom-call | tf_op jit(solution)/shard_map/slamming/pallas_call | solution.py:496
  23.7 0.7 %write_results.1 = (f32[8,64,128]{2,1,0:T(8,128)}, f32[4,128]{1,0:T(4,128)}, f32[4,128]{1,0:T(4,128)}) custom-call(f32[8,64,128]{2,1,0:T(8,128)S(1)} %get-tuple-element.9.p_ref, f32[4,128]{1,0:T(4,128)S(1)} %get-tuple-element.10.plate_ref, f32[4,128]{1,0:T(4,128)S(1)} %get-tuple-element.11.motion_ref), custom_call_target="tpu_custom_call" | custom-call | tf_op jit(solution)/shard_map/write_results/pallas_call | solution.py:537

commit v4 on v2

--- a/solution.py
+++ b/solution.py
@@ -44,7 +44,7 @@
     out_ref, plate_ref, motion_ref,
     p_ref, c_ref, s_ref, small, faces_in,
     pa, pb, wt, xrecv, ysend, yrecv,
-    thin, gbuf, vbuf, ubuf, srecv, lslab, lrecv, win, lwin, onehot, spread, own_hot, uslab,
+    strip, thin, gbuf, vbuf, ubuf, srecv, lslab, lrecv, win, lwin, onehot, spread, own_hot, uslab,
     lsem, fsend, frecv, gsend, grecv, tsend, trecv, rsend, rrecv,
 ):
     nx, ny, nz = p_ref.shape
@@ -198,24 +198,22 @@
             srecv[NEAR + d] = jnp.zeros(srecv.shape[1:], F32)
             lrecv[NEAR + d] = jnp.zeros(lrecv.shape[1:], F32)
 
-    loads_in[0].wait()
-    pack(0)
-    loads_in[1].wait()
-    pack(1)
-    loads_in[2].wait()
-    depth = lax.broadcasted_iota(jnp.int32, (8, nz), 0)
-    layer = lax.broadcasted_iota(jnp.int32, (8, nz), 1)
-    top = jnp.logical_and(depth == layer, depth < 4).astype(F32)
-    low = (depth == layer + 4).astype(F32)
-
-    def take(which, field):
-        return lax.dot_general(
-            which, field[...].reshape(nx * ny, nz), NT, precision=lax.Precision.HIGHEST,
-            preferred_element_type=F32,
-        )
-
-    hull = take(top, p_ref) + take(low, c_ref)
-    feed = take(top, s_ref)
+    for copy in loads_in[:3]:
+        copy.wait()
+    depth = lax.broadcasted_iota(jnp.int32, (8, LANES), 0)
+    along_z = lax.broadcasted_iota(jnp.int32, (ny, nz), 1)
+    for x in range(nx):
+        layers = jnp.where(
+            along_z < 4, p_ref[x], jnp.where(along_z < 8, pltpu.roll(c_ref[x], 4, 1), pltpu.roll(s_ref[x], 8, 1))
+        )
+        for part, value in enumerate(three(layers)):
+            strip[part, x * ny:(x + 1) * ny, :] = value
+    pick = jnp.where(
+        lax.broadcasted_iota(jnp.int32, (16, nz), 0) == lax.broadcasted_iota(jnp.int32, (16, nz), 1), 1.0, 0.0
+    ).astype(BF16)
+    moved = [lax.dot_general(pick, strip[part], NT, preferred_element_type=F32) for part in range(3)]
+    moved = (moved[0] + moved[1]) + moved[2]
+    hull, feed = moved[:8], moved[8:]
     near = lax.broadcasted_iota(jnp.int32, (8, LANES), 1)
     for x in range(nx):
         v = (x // 2) * LANES
@@ -225,11 +223,6 @@
         else:
             one = pltpu.roll(one, ny, 1)
         thin[1, reach + x] = jnp.where(near < ny, one, two)
-    for copy in loads_in[3:]:
-        copy.wait()
-    gbuf[0, c] = (faces_in[0] * (px * py) + faces_in[1]).astype(F32)
-    for f in range(3):
-        gbuf[1 + f, c] = small[f]
 
     pl.semaphore_wait(barrier, peers)
 
@@ -239,8 +232,15 @@
             skin(dr, dc).start()
     halo_start(0, (0, 1))
     halo_start(1, (0, 1))
+    pack(0)
     halo_start(0, (2, 3))
+    pack(1)
     halo_start(1, (2, 3))
+    for copy in loads_in[3:]:
+        copy.wait()
+    gbuf[0, c] = (faces_in[0] * (px * py) + faces_in[1]).astype(F32)
+    for f in range(3):
+        gbuf[1 + f, c] = small[f]
     gather_start(0)
 
     row_id = lax.broadcasted_iota(jnp.int32, (ny, nz), 0)
@@ -300,8 +300,8 @@
         pc = jnp.where(middle, pltpu.roll(own, half, 1), pltpu.roll(side, half + ny, 1))
         side = jnp.where(near >= ny + half, left, right)
         ss.append(jnp.where(middle, pltpu.roll(own, half + ny, 1), pltpu.roll(side, half, 1)))
-        ps.append(jnp.where(depth[:, :LANES] < 4, pc, 0.0))
-        cs.append(jnp.where(depth[:, :LANES] < 4, pltpu.roll(pc, 4, 0), 0.0))
+        ps.append(jnp.where(depth < 4, pc, 0.0))
+        cs.append(jnp.where(depth < 4, pltpu.roll(pc, 4, 0), 0.0))
 
     def thin_six(field, x):
         mid = field[x]
@@ -380,13 +380,12 @@
         lslab[dev] = slab[dev * px:(dev + 1) * px]
     along_each(1, lambda copy: copy.start())
 
-    halo_wait(2, (2, 3))
-    for x in range(1, last):
-        sweep(pa, pb, 2, x)
-    halo_wait(2, (0, 1))
+    halo_wait(2, (0, 1, 2, 3))
     for x in (0, last):
         sweep(pa, pb, 2, x)
     halo_start(3, (0, 1))
+    for x in range(1, last):
+        sweep(pa, pb, 2, x)
     pack(3)
     halo_start(3, (2, 3))
 
@@ -415,6 +414,20 @@
         return 2.0 * now - before - laplace(stiff * laplace(now)) * inverse
 
     ahead = free(current, previous)
+
+    halo_wait(3, (2, 3))
+    for x in range(1, last):
+        sweep(pb, out_ref, 3, x)
+
+    for phase in range(3):
+        halo_sent(phase)
+    for dr, dc in blocks:
+        @pl.when(both_ok(dr, dc))
+        def _(dr=dr, dc=dc):
+            skin(dr, dc).wait_send()
+    for which in range(2):
+        gather_sent(which)
+    along_each(0, lambda copy: copy.wait_send())
 
     along_each(1, lambda copy: copy.wait_recv(), back=True)
     lwin[WIN * px:, :] = jnp.zeros((tall - WIN * px, wide), F32)
@@ -442,22 +455,11 @@
         part = jnp.where(keep, picked[:, j * LANES:(j + 1) * LANES], 0.0)
         motion_ref[j:j + 1, :] = jnp.sum(part, axis=0, keepdims=True)
 
-    halo_wait(3, (2, 3))
-    for x in range(1, last):
-        sweep(pb, out_ref, 3, x)
     halo_wait(3, (0, 1))
     for x in (0, last):
         sweep(pb, out_ref, 3, x)
-
-    for phase in range(4):
-        halo_sent(phase)
-    for dr, dc in blocks:
-        @pl.when(both_ok(dr, dc))
-        def _(dr=dr, dc=dc):
-            skin(dr, dc).wait_send()
-    for which in range(2):
-        gather_sent(which)
-        along_each(which, lambda copy: copy.wait_send())
+    halo_sent(3)
+    along_each(1, lambda copy: copy.wait_send())
 
 
 def write(p_ref, plate_ref, motion_ref, p_out, plate_out, motion_out, sem):
@@ -508,6 +510,7 @@
             pltpu.VMEM((4, 2, ny, nz), F32),
             pltpu.VMEM((4, 2, nx, nz), F32),
             pltpu.VMEM((4, 2, nx, nz), F32),
+            pltpu.VMEM((3, nx * ny, nz), BF16),
             pltpu.VMEM((3, nx + 2 * SWEEPS, 8, LANES), F32),
             pltpu.VMEM((4, cols, px, py), F32),
             pltpu.VMEM((cols, frows, LANES), F32),

time: 21.9 us -> 22.4 us (1.023)
  the two profiles are of different devices: /device:TPU:0 before, /device:TPU:1 now
where the time goes in v4:
time: 22.4 us; the launch traced here: 22.3 us
  Pallas kernels  21.7 us (97%)
  between operations  0.64 us (3%)
    pallas_call x1, Pallas kernels, shards(): pl.pallas_call(functools.partial(kernel, rows, cols), out_shape=tuple((pl...  20.9 us
    pallas_call x1, Pallas kernels, shards(): pl.pallas_call(write, out_shape=shapes, in_specs=[vmem] * 3, out_specs=(h...  0.74 us

profile of v4, /device:TPU:1, one launch (start us, length us, event | category | flops | bytes accessed | tf_op | source)
XLA Modules:
  0.0 22.3 jit_solution(16340680248013762137)
XLA Ops:
  0.6 20.9 %slamming.1 = (f32[8,64,128]{2,1,0:T(8,128)S(1)}, f32[4,128]{1,0:T(4,128)S(1)}, f32[4,128]{1,0:T(4,128)S(1)}) custom-call(f32[8,64,128]{2,1,0:T(8,128)} %p_hbm.1, f32[8,64,128]{2,1,0:T(8,128)} %c_hbm.1, f32[8,64,128]{2,1,0:T(8,128)} %s_hbm.1, f32[4,128]{1,0:T(4,128)} %disp_hbm.1, f32[4,128]{1,0:T(4,128)} %prev_hbm.1, f32[4,128]{1,0:T(4,128)} %thick_hbm.1, ...), custom_call_target="tpu_custom_call" | custom-call | tf_op jit(solution)/shard_map/slamming/pallas_call | solution.py:496
  21.6 0.7 %write_results.1 = (f32[8,64,128]{2,1,0:T(8,128)}, f32[4,128]{1,0:T(4,128)}, f32[4,128]{1,0:T(4,128)}) custom-call(f32[8,64,128]{2,1,0:T(8,128)S(1)} %get-tuple-element.9.p_ref, f32[4,128]{1,0:T(4,128)S(1)} %get-tuple-element.10.plate_ref, f32[4,128]{1,0:T(4,128)S(1)} %get-tuple-element.11.motion_ref), custom_call_target="tpu_custom_call" | custom-call | tf_op jit(solution)/shard_map/write_results/pallas_call | solution.py:538

commit v5 on v4

--- a/solution.py
+++ b/solution.py
@@ -45,7 +45,7 @@
     p_ref, c_ref, s_ref, small, faces_in,
     pa, pb, wt, xrecv, ysend, yrecv,
     strip, thin, gbuf, vbuf, ubuf, srecv, lslab, lrecv, win, lwin, onehot, spread, own_hot, uslab,
-    lsem, fsend, frecv, gsend, grecv, tsend, trecv, rsend, rrecv,
+    lsem, fsend, frecv, gsend, grecv, tsend, trecv, rsend, rrecv, hsend, hrecv,
 ):
     nx, ny, nz = p_ref.shape
     px, py = small.shape[1:]
@@ -153,9 +153,32 @@
     def gather_sent(which):
         times(cols - 1, lambda step: gather(which, step).wait_send())
 
+    core = lax.rem(c, 2)
+    ncol = cols // 2
+
+    def hand(d):
+        half = srecv.at[NEAR + d, :, pl.ds(core * ncol, ncol)]
+        return pltpu.make_async_remote_copy(
+            src_ref=half, dst_ref=half, send_sem=hsend.at[NEAR + d], recv_sem=hrecv.at[NEAR + d],
+            device_id=(r, c + 1 - 2 * core), device_id_type=MESH,
+        )
+
+    def handed(d):
+        half = srecv.at[NEAR + d, :, pl.ds((1 - core) * ncol, ncol)]
+        return pltpu.make_async_remote_copy(
+            src_ref=half, dst_ref=half, send_sem=hsend.at[NEAR + d], recv_sem=hrecv.at[NEAR + d],
+            device_id=(r, c + 1 - 2 * core), device_id_type=MESH,
+        )
+
+    def hand_each(act, which):
+        for d in shifts:
+            @pl.when(row_ok(d))
+            def _(d=d):
+                act(which(d))
+
     def along(which, d):
-        src = gbuf.at[pl.ds(1, 3)] if which == 0 else lslab
-        dst = (srecv if which == 0 else lrecv).at[NEAR - d]
+        src = gbuf.at[pl.ds(1, 3), pl.ds(core * ncol, ncol)] if which == 0 else lslab
+        dst = srecv.at[NEAR - d, :, pl.ds(core * ncol, ncol)] if which == 0 else lrecv.at[NEAR - d]
         return pltpu.make_async_remote_copy(
             src_ref=src, dst_ref=dst, send_sem=rsend.at[which, NEAR - d], recv_sem=rrecv.at[which, NEAR - d],
             device_id=(r + d, c), device_id_type=MESH,
@@ -380,6 +403,9 @@
         lslab[dev] = slab[dev * px:(dev + 1) * px]
     along_each(1, lambda copy: copy.start())
 
+    along_each(0, lambda copy: copy.wait_recv(), back=True)
+    hand_each(lambda copy: copy.start(), hand)
+
     halo_wait(2, (0, 1, 2, 3))
     for x in (0, last):
         sweep(pa, pb, 2, x)
@@ -389,7 +415,7 @@
     pack(3)
     halo_start(3, (2, 3))
 
-    along_each(0, lambda copy: copy.wait_recv(), back=True)
+    hand_each(lambda copy: copy.wait_recv(), handed)
     tall, wide = lwin.shape
     win[:, WIN * px:, :] = jnp.zeros((3, tall - WIN * px, wide), F32)
     for w in range(WIN):
@@ -428,6 +454,7 @@
     for which in range(2):
         gather_sent(which)
     along_each(0, lambda copy: copy.wait_send())
+    hand_each(lambda copy: copy.wait_send(), hand)
 
     along_each(1, lambda copy: copy.wait_recv(), back=True)
     lwin[WIN * px:, :] = jnp.zeros((tall - WIN * px, wide), F32)
@@ -476,7 +503,7 @@
     px, py = disp.shape
     faces = elem.shape[0]
     frows = faces // LANES
-    assert LANES == 2 * ny and nz == LANES and py == LANES
+    assert cols % 2 == 0 and LANES == 2 * ny and nz == LANES and py == LANES
     high = cols * px
     tall = -(-WIN * px // 8) * 8
     chunk = 8 if cols % 8 == 0 else 1
@@ -529,6 +556,7 @@
             dma((2, cols - 1)), dma((2, cols - 1)),
             dma((9,)), dma((9,)),
             dma((2, WIN)), dma((2, WIN)),
+            dma((WIN,)), dma((WIN,)),
         ],
         compiler_params=pltpu.CompilerParams(
             collective_id=0, has_side_effects=True, vmem_limit_bytes=48 * 1024 * 1024

time: 22.4 us -> 22.1 us (0.987)
  the two profiles are of different devices: /device:TPU:1 before, /device:TPU:0 now
where the time goes in v5:
time: 22.1 us; the launch traced here: 22 us
  Pallas kernels  21.3 us (96%)
  between operations  0.64 us (3%)
    pallas_call x1, Pallas kernels, shards(): pl.pallas_call(functools.partial(kernel, rows, cols), out_shape=tuple((pl...  20.6 us
    pallas_call x1, Pallas kernels, shards(): pl.pallas_call(write, out_shape=shapes, in_specs=[vmem] * 3, out_specs=(h...  0.74 us

profile of v5, /device:TPU:0, one launch (start us, length us, event | category | flops | bytes accessed | tf_op | source)
XLA Modules:
  0.0 22.0 jit_solution(14694679201171660781)
XLA Ops:
  0.6 20.6 %slamming.1 = (f32[8,64,128]{2,1,0:T(8,128)S(1)}, f32[4,128]{1,0:T(4,128)S(1)}, f32[4,128]{1,0:T(4,128)S(1)}) custom-call(f32[8,64,128]{2,1,0:T(8,128)} %p_hbm.1, f32[8,64,128]{2,1,0:T(8,128)} %c_hbm.1, f32[8,64,128]{2,1,0:T(8,128)} %s_hbm.1, f32[4,128]{1,0:T(4,128)} %disp_hbm.1, f32[4,128]{1,0:T(4,128)} %prev_hbm.1, f32[4,128]{1,0:T(4,128)} %thick_hbm.1, ...), custom_call_target="tpu_custom_call" | custom-call | tf_op jit(solution)/shard_map/slamming/pallas_call | solution.py:523
  21.2 0.7 %write_results.1 = (f32[8,64,128]{2,1,0:T(8,128)}, f32[4,128]{1,0:T(4,128)}, f32[4,128]{1,0:T(4,128)}) custom-call(f32[8,64,128]{2,1,0:T(8,128)S(1)} %get-tuple-element.9.p_ref, f32[4,128]{1,0:T(4,128)S(1)} %get-tuple-element.10.plate_ref, f32[4,128]{1,0:T(4,128)S(1)} %get-tuple-element.11.motion_ref), custom_call_target="tpu_custom_call" | custom-call | tf_op jit(solution)/shard_map/write_results/pallas_call | solution.py:566
